TPU v7x, 1024 devices: a whole 4x8x16 slice. The times are simulated.
1024 devices in a mesh: dp: 16 (over z), expert: 16 (over y, core), tensor: 4 (over x).
Axes of the slice: x: 4, y: 8, z: 16, core: 2. Of those that a mesh axis runs over, the one named last changes fastest.
Arguments:
- grad_out: bfloat16 [32768, 1792], P(('dp', 'expert')), may hold values from -6 to 6
- expert_ids: int32 [32768, 8], P(('dp', 'expert')), may hold values from 0 to 63, all different within a row; in each aligned block of 32 rows (0 to 31, 32 to 63, ...) at most 6 rows name the same one
- gate_probs: float32 [32768, 8], P(('dp', 'expert')), may hold values from 0.1 to 0.6
- saved_inputs: bfloat16 [16, 16, 4, 16, 6, 1792], P('dp', 'expert'), may hold values from -6 to 6
- w_gate: bfloat16 [16, 1792, 1280], P('expert', None, 'tensor'), may hold values from -0.125 to 0.125
- w_up: bfloat16 [16, 1792, 1280], P('expert', None, 'tensor'), may hold values from -0.125 to 0.125
- w_down: bfloat16 [16, 1792, 1280], P('expert', None, 'tensor'), may hold values from -0.15625 to 0.15625
Outputs:
- input_grad: bfloat16 [32768, 1792], P(('dp', 'expert'))
- prob_grad: float32 [32768, 8], P(('dp', 'expert'))
- gate_weight_grad: float32 [16, 1792, 1280], P('expert', 'dp', 'tensor')
- up_weight_grad: float32 [16, 1792, 1280], P('expert', 'dp', 'tensor')
- down_weight_grad: float32 [16, 1792, 1280], P('expert', 'dp', 'tensor')
Inputs may be any that keep to these rules, and one draw needn't show every extreme that they name: `expert_ids`: each row names 8 different experts; in every aligned block of 32 rows no expert is named by more than 6 rows.
All inputs are finite; a program needn't handle non-finite values.
Results may differ from a plain program's by a relative error of at most 0.02.
Values may be sent and summed in bfloat16 or wider, within the bound.
A program may use at most 64 MiB of HBM per device.

v0:
```python
import jax
import jax.numpy as jnp
from jax import lax
from jax.sharding import PartitionSpec as P

EXP_DEV = 4


def silu_parts(pre_gate):
    sigmoid_val = jax.nn.sigmoid(pre_gate)
    return (pre_gate * sigmoid_val, sigmoid_val * (1.0 + pre_gate * (1.0 - sigmoid_val)))


def contract_rows(left, right):
    return lax.dot_general(
        left, right, (((0,), (0,)), ((), ())), preferred_element_type=jnp.float32
    )


def contract_hidden(left, right):
    return lax.dot_general(
        left, right, (((1,), (1,)), ((), ())), preferred_element_type=jnp.float32
    )


def column_term(left, right):
    return contract_rows(left, right)


def shards(grad_out, expert_ids, gate_probs, saved_inputs, w_gate, w_up, w_down):
    n_tensor = lax.axis_size("tensor")
    n_expert = lax.axis_size("expert")
    tok_rows, model_width = grad_out.shape
    share_rows = tok_rows // n_tensor
    capacity = saved_inputs.shape[4]
    top_count = expert_ids.shape[1]
    hidden_width = w_gate.shape[2]
    positions = jnp.arange(n_expert, dtype=jnp.int32)
    onehot = (
        (expert_ids[:, :, None] // EXP_DEV == positions) & (expert_ids[:, :, None] % EXP_DEV == 0)
    ).astype(jnp.int32)
    routed = jnp.sum(onehot, axis=1)
    blocked = routed.reshape(n_tensor, share_rows, n_expert)
    slot_rank = jnp.cumsum(blocked, axis=1) - blocked
    slot_iota = jnp.arange(capacity, dtype=jnp.int32)
    placed = (blocked[..., None] * (slot_rank[..., None] == slot_iota).astype(jnp.int32)).astype(
        jnp.bfloat16
    )
    prob_tok = jnp.sum(onehot.astype(jnp.float32) * gate_probs[:, :, None], axis=1).astype(
        jnp.bfloat16
    )
    prob_tok = prob_tok.reshape(n_tensor, share_rows, n_expert)
    grad_blocks = grad_out.reshape(n_tensor, share_rows, model_width)
    send_grad = jnp.einsum(
        "tipc,tid->tpcd", placed, grad_blocks, preferred_element_type=jnp.float32
    ).astype(jnp.bfloat16)
    send_prob = jnp.sum(placed * prob_tok[..., None], axis=1)
    own_index = lax.axis_index("tensor")
    recv_grad, recv_prob = (
        lax.all_to_all(send_grad, "expert", split_axis=1, concat_axis=1, tiled=True),
        lax.all_to_all(send_prob, "expert", split_axis=1, concat_axis=1, tiled=True),
    )
    slot_count = n_tensor * n_expert * capacity
    inputs = saved_inputs.reshape(slot_count, model_width)
    slot_grads = recv_grad.reshape(slot_count, model_width)
    weights = recv_prob.reshape(slot_count).astype(jnp.float32)[:, None]
    gate_weight = w_gate[0]
    up_weight = w_up[0]
    down_weight = w_down[0]
    pre_gate = jnp.dot(inputs, gate_weight, preferred_element_type=jnp.float32)
    pre_up = jnp.dot(inputs, up_weight, preferred_element_type=jnp.float32)
    silu_val, silu_slope = silu_parts(pre_gate)
    hidden = (silu_val * pre_up).astype(jnp.bfloat16)
    scaled = (weights * slot_grads.astype(jnp.float32)).astype(jnp.bfloat16)
    backward = jnp.dot(slot_grads, down_weight, preferred_element_type=jnp.float32)
    prob_part = jnp.sum(hidden.astype(jnp.float32) * backward, axis=1)
    hidden_grad = weights * backward
    gate_grad = (hidden_grad * pre_up * silu_slope).astype(jnp.bfloat16)
    up_grad = (hidden_grad * silu_val).astype(jnp.bfloat16)
    input_part = contract_hidden(gate_grad, gate_weight) + contract_hidden(up_grad, up_weight)
    input_sum, prob_sum = (
        lax.psum_scatter(
            input_part.reshape(n_tensor, n_expert, capacity, model_width).astype(jnp.bfloat16),
            "tensor",
            scatter_dimension=0,
            tiled=True,
        ).astype(jnp.float32),
        lax.psum_scatter(
            prob_part.reshape(n_tensor, n_expert, capacity).astype(jnp.bfloat16),
            "tensor",
            scatter_dimension=0,
            tiled=True,
        ).astype(jnp.float32),
    )
    gate_and_up = jnp.concatenate([gate_grad, up_grad], axis=1)
    ret_grad, ret_prob = (
        lax.all_to_all(
            input_sum.astype(jnp.bfloat16), "expert", split_axis=1, concat_axis=1, tiled=True
        ),
        lax.all_to_all(
            prob_sum.astype(jnp.bfloat16), "expert", split_axis=1, concat_axis=1, tiled=True
        ),
    )
    own_placed = lax.dynamic_slice_in_dim(placed, own_index, 1, 0)[0]
    input_share = jnp.einsum(
        "ipc,pcd->id", own_placed, ret_grad[0], preferred_element_type=jnp.float32
    ).astype(jnp.bfloat16)
    prob_pos = jnp.einsum("ipc,pc->ip", own_placed, ret_prob[0], preferred_element_type=jnp.float32)
    own_onehot = lax.dynamic_slice_in_dim(
        onehot.reshape(n_tensor, share_rows, top_count, n_expert), own_index, 1, 0
    )[0]
    prob_share = jnp.sum(own_onehot.astype(jnp.float32) * prob_pos[:, None, :], axis=2).astype(
        jnp.bfloat16
    )
    input_full, prob_full = (
        lax.all_gather(input_share, "tensor", axis=0, tiled=True),
        lax.all_gather(prob_share, "tensor", axis=0, tiled=True),
    )
    first = column_term(inputs, gate_and_up)
    second = column_term(scaled, hidden)
    summed = lax.psum_scatter(
        jnp.concatenate([first, second], axis=1).astype(jnp.bfloat16),
        "dp",
        scatter_dimension=0,
        tiled=True,
    ).astype(jnp.float32)
    gate_shard = summed[:, :hidden_width]
    up_shard = summed[:, hidden_width : 2 * hidden_width]
    down_shard = summed[:, 2 * hidden_width :]
    return (
        input_full,
        prob_full.astype(jnp.float32),
        gate_shard[None],
        up_shard[None],
        down_shard[None],
    )


def solution(mesh):
    return jax.shard_map(
        shards,
        mesh=mesh,
        in_specs=(
            P(("dp", "expert"), None),
            P(("dp", "expert"), None),
            P(("dp", "expert"), None),
            P("dp", "expert", None, None, None, None),
            P("expert", None, "tensor"),
            P("expert", None, "tensor"),
            P("expert", None, "tensor"),
        ),
        out_specs=(
            P(("dp", "expert"), None),
            P(("dp", "expert"), None),
            P("expert", "dp", "tensor"),
            P("expert", "dp", "tensor"),
            P("expert", "dp", "tensor"),
        ),
        check_vma=False,
    )
```

profile of v0, /device:TPU:12, one launch (start us, length us, event | category | flops | bytes accessed | tf_op | source)
XLA Modules:
  0.0 244.2 jit_solution(14060295280126980527)
XLA Ops:
  7.2 0.8 fusion.26
  8.0 0.7 add_select_fusion.1
  8.7 0.7 fusion.20
  9.4 0.1 convert_element_type.95
  9.5 0.1 copy.97
  9.6 0.1 copy.99
  9.7 0.1 reduce_window_sum.14
  9.8 0.1 copy.98
  9.8 0.1 multiply_reduce_fusion.1
  10.0 0.7 copy.101
  10.7 7.6 %all-to-all-start = ((bf16[4,16,6]{2,0,1:T(4,128)(2,1)}), bf16[4,16,6]{2,0,1:T(4,128)(2,1)S(1)}, u32[]{:S(2)}, u32[]{:S(2)}) async-start(bf16[4,16,6]{2,0,1:T(4,128)(2,1)} %copy.101), calls=%async_computation | async-start | bytes 32768 | tf_op jit(solution)/shard_map/all_to_all | solution.py:61
  18.3 1.5 convolution_convert_fusion.1
  19.8 2.1 copy.104
  21.9 2.6 %all-to-all-done = bf16[4,16,6]{2,0,1:T(4,128)(2,1)S(1)} async-done(((bf16[4,16,6]{2,0,1:T(4,128)(2,1)}), bf16[4,16,6]{2,0,1:T(4,128)(2,1)S(1)}, u32[]{:S(2)}, u32[]{:S(2)}) %all-to-all-start) | async-done | bytes 800 | tf_op jit(solution)/shard_map/all_to_all | solution.py:61
  24.5 5.6 %all-to-all-start.1 = ((bf16[4,16,6,1792]{3,0,2,1:T(4,128)(2,1)}), bf16[4,16,6,1792]{3,0,2,1:T(4,128)(2,1)}, u32[]{:S(2)}, u32[]{:S(2)}) async-start(bf16[4,16,6,1792]{3,0,2,1:T(4,128)(2,1)} %copy.104), calls=%async_computation.1 | async-start | bytes 2752512 | tf_op jit(solution)/shard_map/all_to_all | solution.py:60
  30.1 0.0 reduce-scatter.8.cloned.1.call-start
  30.2 1.8 copy.106
  32.0 1.3 reshape.86
  33.3 3.1 %fusion.6 = f32[384,320]{0,1:T(8,128)} fusion(bf16[384,1792]{1,0:T(8,128)(2,1)} %reshape.86, bf16[1,1792,320]{1,2,0:T(8,128)(2,1)S(1)} %copy-done), kind=kOutput, calls=%fused_computation.13 | convolution fusion | flops 440401920 | bytes 3014656 | tf_op jit(solution)/shard_map/dot_general | solution.py:70
  36.4 1.5 fusion.9
  37.9 0.1 copy.102
  38.0 0.1 copy.103
  38.2 0.1 reshape.87
  38.3 23.8 %all-to-all-done.1 = bf16[4,16,6,1792]{3,0,2,1:T(4,128)(2,1)} async-done(((bf16[4,16,6,1792]{3,0,2,1:T(4,128)(2,1)}), bf16[4,16,6,1792]{3,0,2,1:T(4,128)(2,1)}, u32[]{:S(2)}, u32[]{:S(2)}) %all-to-all-start.1) | async-done | bytes 1376288 | tf_op jit(solution)/shard_map/all_to_all | solution.py:60
  62.1 1.5 copy.105
  63.6 1.4 reshape.85
  65.0 2.9 %multiply_reduce_fusion = (bf16[384]{0:T(512)(128)(2,1)S(1)}, bf16[384,320]{0,1:T(8,128)(2,1)S(1)}, bf16[384,320]{0,1:T(8,128)(2,1)S(1)}, bf16[384,320]{0,1:T(8,128)(2,1)S(1)}) fusion(f32[384,320]{0,1:T(8,128)} %fusion.9, f32[384,320]{0,1:T(8,128)} %fusion.6, f32[384]{0:T(512)S(1)} %reshape.87, bf16[384,1792]{1,0:T(8,128)(2,1)} %reshape.85, ...), kind=kOutput, calls=%fused_computation.23 | convolution fusion | flops 442736256 | bytes 4245760 | tf_op jit(solution)/shard_map/dot_general | solution.py:75
  67.8 0.8 convert_element_type.110
  68.6 0.0 reduce-scatter.8.cloned.1.call-update
  68.6 0.0 reduce-scatter.6.cloned.1.call-start
  68.7 0.9 fusion.4
  69.6 0.3 copy-done.5
  69.9 0.9 fusion.1
  70.9 1.6 convert_element_type.102
  72.4 0.0 reduce-scatter.6.cloned.1.call-update
  72.5 0.0 reduce-scatter.10.cloned.1.call-start
  72.5 1.3 copy-done.3
  73.8 0.9 convolution_convert_fusion.2
  74.7 0.5 copy-done.2
  75.1 1.4 fusion
  76.5 2.0 pad_maximum_fusion
  78.5 5.9 %copy.118 = bf16[1792,960]{1,0:T(8,128)(2,1)} copy(bf16[1792,960]{0,1:T(8,128)(2,1)} %pad_maximum_fusion) | data formatting | bytes 6881280
  84.4 0.0 reduce-scatter.10.cloned.1.call-update
  84.4 0.1 and.33
  84.5 0.1 eq.49
  84.6 20.3 %reduce-scatter.8.cloned.1.call-done = bf16[1,16,6]{2,1,0:T(8,128)(2,1)} async-done(((bf16[4,16,6]{2,1,0:T(8,128)(2,1)}), bf16[1,16,6]{2,1,0:T(8,128)(2,1)}) %reduce-scatter.8.cloned.1.call-update) | async-done | bytes 208 | tf_op jit(solution)/shard_map/reduce_scatter | solution.py:88
  104.9 1.3 copy.111
  106.2 7.3 %all-to-all-start.3 = ((bf16[1,16,6]{2,0,1:T(2,128)(2,1)}), bf16[1,16,6]{2,0,1:T(2,128)(2,1)S(1)}, u32[]{:S(2)}, u32[]{:S(2)}) async-start(bf16[1,16,6]{2,0,1:T(2,128)(2,1)} %copy.111), calls=%async_computation.5 | async-start | bytes 16384 | tf_op jit(solution)/shard_map/all_to_all | solution.py:100
  113.5 6.1 %all-to-all-done.3 = bf16[1,16,6]{2,0,1:T(2,128)(2,1)S(1)} async-done(((bf16[1,16,6]{2,0,1:T(2,128)(2,1)}), bf16[1,16,6]{2,0,1:T(2,128)(2,1)S(1)}, u32[]{:S(2)}, u32[]{:S(2)}) %all-to-all-start.3) | async-done | bytes 224 | tf_op jit(solution)/shard_map/all_to_all | solution.py:100
  119.6 27.3 %reduce-scatter.6.cloned.1.call-done = bf16[1,16,6,1792]{3,2,1,0:T(8,128)(2,1)} async-done(((bf16[4,16,6,1792]{3,2,1,0:T(8,128)(2,1)}), bf16[1,16,6,1792]{3,2,1,0:T(8,128)(2,1)}) %reduce-scatter.6.cloned.1.call-update) | async-done | bytes 344080 | tf_op jit(solution)/shard_map/reduce_scatter | solution.py:82
  146.9 7.3 %all-to-all-start.2 = ((bf16[1,16,6,1792]{3,2,0,1:T(8,128)(2,1)}), bf16[1,16,6,1792]{3,2,0,1:T(8,128)(2,1)S(1)}, u32[]{:S(2)}, u32[]{:S(2)}) async-start(bf16[1,16,6,1792]{3,2,0,1:T(8,128)(2,1)} %bitcast.74), calls=%async_computation.3 | async-start | bytes 917504 | tf_op jit(solution)/shard_map/all_to_all | solution.py:97
  154.2 0.1 copy.112
  154.3 0.1 copy.115
  154.4 0.1 fusion.24
  154.6 0.1 fusion.21
  154.6 11.3 %all-gather = bf16[4,32,8]{1,2,0:T(8,128)(2,1)S(1)} all-gather(bf16[1,32,8]{1,2,0:T(8,128)(2,1)S(1)} %bitcast.76), channel_id=1, replica_groups=mesh['dp'=16,'expert'=16,'tensor'=4] {'tensor'}, dimensions={0}, use_global_device_ids=true | all-gather | bytes 2560 | tf_op jit(solution)/shard_map/all_gather | solution.py:117
  165.9 0.7 reshape.90
  166.6 0.6 all-to-all-done.2
  167.2 0.2 fusion.2
  167.4 12.9 %all_gather.6 = bf16[128,1792]{1,0:T(8,128)(2,1)S(1)} all-gather(bf16[32,1792]{1,0:T(8,128)(2,1)S(1)} %fusion.2), channel_id=1, replica_groups=mesh['dp'=16,'expert'=16,'tensor'=4] {'tensor'}, dimensions={0}, use_global_device_ids=true | all-gather | bytes 573440 | tf_op jit(solution)/shard_map/all_gather | solution.py:116
  180.3 54.6 %reduce-scatter.10.cloned.1.call-done = bf16[112,960]{1,0:T(8,128)(2,1)} async-done(((bf16[1792,960]{1,0:T(8,128)(2,1)}), bf16[112,960]{1,0:T(8,128)(2,1)}) %reduce-scatter.10.cloned.1.call-update) | async-done | bytes 215056
  234.9 1.1 copy.119
  236.1 0.8 slice_bitcast_fusion
  236.9 0.8 copy.127
  (20 shorter events, 0.2 us)
Async XLA Ops:
  7.2 26.1 %copy-start = (bf16[1,1792,320]{1,2,0:T(8,128)(2,1)S(1)}, bf16[1,1792,320]{1,2,0:T(8,128)(2,1)}, u32[]{:S(2)}) copy-start(bf16[1,1792,320]{1,2,0:T(8,128)(2,1)} %param.11) | copy-start | bytes 3440644
  10.7 13.8 %all-to-all-start = ((bf16[4,16,6]{2,0,1:T(4,128)(2,1)}), bf16[4,16,6]{2,0,1:T(4,128)(2,1)S(1)}, u32[]{:S(2)}, u32[]{:S(2)}) async-start(bf16[4,16,6]{2,0,1:T(4,128)(2,1)} %copy.101), calls=%async_computation | async-start | bytes 32768 | tf_op jit(solution)/shard_map/all_to_all | solution.py:61
  24.5 37.5 %all-to-all-start.1 = ((bf16[4,16,6,1792]{3,0,2,1:T(4,128)(2,1)}), bf16[4,16,6,1792]{3,0,2,1:T(4,128)(2,1)}, u32[]{:S(2)}, u32[]{:S(2)}) async-start(bf16[4,16,6,1792]{3,0,2,1:T(4,128)(2,1)} %copy.104), calls=%async_computation.1 | async-start | bytes 2752512 | tf_op jit(solution)/shard_map/all_to_all | solution.py:60
  30.1 74.7 %reduce-scatter.8.cloned.1.call-start = ((), (), s32[]{:S(2)}) async-start(), calls=%async_computation.8 | async-start | bytes 20480 | tf_op jit(solution)/shard_map/reduce_scatter | solution.py:88
  33.3 3.1 %copy-start.1 = (bf16[384,1792]{1,0:T(8,128)(2,1)S(1)}, bf16[384,1792]{1,0:T(8,128)(2,1)}, u32[]{:S(2)}) copy-start(bf16[384,1792]{1,0:T(8,128)(2,1)} %reshape.86) | copy-start | bytes 4128772
  33.3 3.1 %copy-start.4 = (bf16[1,1792,320]{1,2,0:T(8,128)(2,1)S(1)}, bf16[1,1792,320]{1,2,0:T(8,128)(2,1)}, u32[]{:S(2)}) copy-start(bf16[1,1792,320]{1,2,0:T(8,128)(2,1)} %param.12) | copy-start | bytes 3440644
  68.6 78.3 %reduce-scatter.6.cloned.1.call-start = ((), (), s32[]{:S(2)}) async-start(), calls=%async_computation.7 | async-start | bytes 2293760 | tf_op jit(solution)/shard_map/reduce_scatter | solution.py:82
  68.7 1.3 copy-start.5
  72.4 1.3 copy-start.3
  72.5 162.4 %reduce-scatter.10.cloned.1.call-start = ((), (), s32[]{:S(2)}) async-start(), calls=%async_computation.9 | async-start | bytes 3899392
  73.8 1.3 copy-start.2
  106.2 13.4 %all-to-all-start.3 = ((bf16[1,16,6]{2,0,1:T(2,128)(2,1)}), bf16[1,16,6]{2,0,1:T(2,128)(2,1)S(1)}, u32[]{:S(2)}, u32[]{:S(2)}) async-start(bf16[1,16,6]{2,0,1:T(2,128)(2,1)} %copy.111), calls=%async_computation.5 | async-start | bytes 16384 | tf_op jit(solution)/shard_map/all_to_all | solution.py:100
  146.9 20.3 %all-to-all-start.2 = ((bf16[1,16,6,1792]{3,2,0,1:T(8,128)(2,1)}), bf16[1,16,6,1792]{3,2,0,1:T(8,128)(2,1)S(1)}, u32[]{:S(2)}, u32[]{:S(2)}) async-start(bf16[1,16,6,1792]{3,2,0,1:T(8,128)(2,1)} %bitcast.74), calls=%async_computation.3 | async-start | bytes 917504 | tf_op jit(solution)/shard_map/all_to_all | solution.py:97
Sparse Core Ops, SparseCore 0:
  68.7 36.0 reduce-scatter.7
  108.7 38.1 reduce-scatter.5
  150.7 84.1 reduce-scatter.9
where the time goes:
time: 245 us; the launch traced here: 244 us
  waiting for transfers between devices  135 us (55%)
  starting transfers between devices  27.9 us (11%)
  local copies, waits for them, and re-layouts  24.9 us (10%)
  blocking collectives  24.2 us (10%)
  between operations  13.9 us (6%)
  matrix products  13.4 us (5%)
  other arithmetic  4.56 us (2%)
    unnamed x4, waiting for transfers between devices  54.6 us
    reduce_scatter x1, waiting for transfers between devices, shards(): lax.psum_scatter(input_part.reshape(n_tensor, n_expert, capacity, model_w...  27.3 us
    all_to_all x1, waiting for transfers between devices, shards(): lax.all_to_all(send_grad, 'expert', split_axis=1, concat_axis=1, tiled=True)  23.8 us
    reduce_scatter x1, waiting for transfers between devices, shards(): lax.psum_scatter(prob_part.reshape(n_tensor, n_expert, capacity).astype(j...  20.3 us
    all_gather x1, blocking collectives, shards(): lax.all_gather(input_share, 'tensor', axis=0, tiled=True)  12.9 us
    unnamed x16, local copies, waits for them, and re-layouts  11.6 us
    all_gather x1, blocking collectives, shards(): lax.all_gather(prob_share, 'tensor', axis=0, tiled=True)  11.3 us
    all_to_all x1, starting transfers between devices, shards(): lax.all_to_all(send_prob, 'expert', split_axis=1, concat_axis=1, tiled=True)  7.56 us
  transfers between devices with their start and end apart: 7, of which 7 were waited for; matrix products, arithmetic and copies ran while one was open for 11% of the time, Pallas kernels for 0%

commit v1 on v0

v1 whole, which is shorter than its diff:
```python
import jax
import jax.numpy as jnp
from jax import lax
from jax.experimental import pallas as pl
from jax.experimental.pallas import tpu as pltpu
from jax.sharding import PartitionSpec as P

EXP_DEV = 4
LANES = 256
CHUNK = 48
F32 = jnp.float32
BF16 = jnp.bfloat16
MESH = pl.DeviceIdType.MESH


def dot(left, right, dims=((1,), (0,))):
    return lax.dot_general(left, right, (dims, ((), ())), preferred_element_type=F32)


def iota(shape, dim):
    return lax.broadcasted_iota(jnp.int32, shape, dim)


def unpack_matrices(cap, pieces, n_exp):
    rows = n_exp * CHUNK
    at = iota((1, rows), 1)
    src = sum((at >= CHUNK * m).astype(jnp.int32) for m in range(1, n_exp))
    rest = at - CHUNK * src
    unpack = iota((rows, rows), 0) == rest * n_exp + src
    src = at % n_exp
    pack = iota((rows, rows), 0) == src * CHUNK + at // n_exp
    return unpack, pack


def kernel(
    sizes,
    grad_hbm, ids_hbm, probs_hbm, x_hbm, wg_hbm, wu_hbm, wd_hbm,
    out_ref, prob_out, gate_out, up_out, down_out,
    grad_v, ids_v, probs_v, xb, wg, wu, wd, ids_s, probs_s, prob_all, unpack, pack,
    send_buf, recv_buf, place, place_t,
    xt, slope_up, silu_s, hid_s, dy, scaled, gate_g, up_g, prob_s,
    xs_opp, xs_left, xs_right, xr1, xr2, ret_send, ret_recv, gather,
    dw, zbuf,
    load_sem, ysend, yrecv, xsend, xrecv, rsend, rrecv, wsend, wrecv, gsend, grecv, zsend, zrecv,
):
    n_dp, n_exp, n_ten, cap, top, d, hid = sizes
    share = grad_v.shape[0]
    pieces = d // LANES
    group = n_exp // 4
    slots = n_exp * cap
    half = slots // 2
    g, q, t = lax.axis_index("dp"), lax.axis_index("expert"), lax.axis_index("tensor")
    t_right, t_left, t_opp = (t + 1) % n_ten, (t + n_ten - 1) % n_ten, (t + 2) % n_ten
    g_right, g_left = (g + 1) % n_dp, (g + n_dp - 1) % n_dp

    def remote(src, dst, send, recv, axis, where):
        return pltpu.make_async_remote_copy(
            src_ref=src, dst_ref=dst, send_sem=send, recv_sem=recv,
            device_id={axis: where}, device_id_type=MESH,
        )

    tok = pl.ds(pl.multiple_of(t * share, share), share)
    loads = [
        pltpu.make_async_copy(ids_hbm, ids_v, load_sem.at[0]),
        pltpu.make_async_copy(probs_hbm, probs_v, load_sem.at[1]),
        pltpu.make_async_copy(grad_hbm.at[tok], grad_v, load_sem.at[2]),
        pltpu.make_async_copy(x_hbm, xb, load_sem.at[3]),
        pltpu.make_async_copy(wg_hbm, wg, load_sem.at[4]),
        pltpu.make_async_copy(wu_hbm, wu, load_sem.at[5]),
        pltpu.make_async_copy(wd_hbm, wd, load_sem.at[6]),
    ]
    for load in loads:
        load.start()
    barrier = pltpu.get_barrier_semaphore()

    def greet(k, carry):
        pl.semaphore_signal(barrier, inc=1, device_id={"expert": (q + k) % n_exp}, device_id_type=MESH)
        return carry

    lax.fori_loop(1, n_exp, greet, 0)
    for axis, where in (("tensor", t_right), ("tensor", t_left), ("dp", g_right), ("dp", g_left)):
        pl.semaphore_signal(barrier, inc=1, device_id={axis: where}, device_id_type=MESH)

    loads[0].wait()
    loads[1].wait()
    tokens_all = ids_s.shape[0]
    fill = jnp.zeros((128 - top, tokens_all), F32)
    ids_s[...] = jnp.concatenate([ids_v[...].astype(F32), fill], axis=0).T
    probs_s[...] = jnp.concatenate([probs_v[...], fill], axis=0).T
    ids = ids_s[tok, :]
    probs = probs_s[tok, :]
    lane = iota((share, 128), 1)
    name = (lane * EXP_DEV).astype(F32)
    routed = jnp.zeros((share, 128), F32)
    prob_tok = jnp.zeros((share, 128), F32)
    for k in range(top):
        hit = ids[:, k : k + 1] == name
        routed = routed + jnp.where(hit, 1.0, 0.0)
        prob_tok = prob_tok + jnp.where(hit, probs[:, k : k + 1], 0.0)
    lower = jnp.where(iota((share, share), 1) < iota((share, share), 0), 1.0, 0.0).astype(BF16)
    rank = dot(lower, routed.astype(BF16))
    code = jnp.where(routed > 0.0, rank, -128.0).astype(BF16)
    spread = ((iota((share, LANES), 1) % share) == iota((share, LANES), 0)).astype(BF16)
    code_x = dot(code, spread, ((0,), (0,)))
    rule = (iota((CHUNK, LANES), 0) - cap * (iota((CHUNK, LANES), 1) // share)).astype(F32)
    for p in range(n_exp):
        place[CHUNK * p : CHUNK * (p + 1), :] = jnp.where(code_x[p : p + 1, :] == rule, 1.0, 0.0).astype(BF16)
    loads[2].wait()
    grad = grad_v[...]
    stacked = jnp.concatenate(
        [grad[:, LANES * j : LANES * (j + 1)] for j in range(pieces)]
        + [jnp.concatenate([prob_tok, jnp.zeros((share, LANES - 128), F32)], axis=1).astype(BF16)],
        axis=0,
    )
    send_buf[...] = dot(place[...], stacked).astype(BF16).reshape(n_exp, CHUNK, LANES)
    pl.semaphore_wait(barrier, n_exp + 3)

    def partner(i):
        step = i // 2 + 1
        return (q + (i % 2) * (n_exp - 2 * step) + step) % n_exp

    def ycopy(i):
        p = partner(i)
        return remote(send_buf.at[p], recv_buf.at[0, q], ysend.at[p], yrecv.at[q], "expert", p)

    def ystart(i, carry):
        ycopy(i).start()
        return carry

    lax.fori_loop(0, n_exp - 1, ystart, 0)
    recv_buf[0, pl.ds(q, 1)] = send_buf[pl.ds(q, 1)]

    mine = q // group
    order = [mine, (mine + 1) % 4, (mine + 3) % 4, (mine + 2) % 4]

    def members(i):
        return pl.ds(order[i] * group, group)

    def ywait(i):
        def one(m, carry):
            src = order[i] * group + m

            @pl.when(src != q)
            def _():
                remote(send_buf.at[src], recv_buf.at[0, src], ysend.at[src], yrecv.at[src], "expert", src).wait_recv()

            return carry

        lax.fori_loop(0, group, one, 0)

    def xcopy(kind, i):
        m = members(i)
        if kind == 0:
            return remote(recv_buf.at[0, m], recv_buf.at[1, m], xsend.at[0, i], xrecv.at[0, i], "tensor", t_right)
        if kind == 1:
            return remote(recv_buf.at[0, m], recv_buf.at[2, m], xsend.at[1, i], xrecv.at[1, i], "tensor", t_left)
        if i < 2:
            return remote(recv_buf.at[1, m], recv_buf.at[3, m], xsend.at[2, i], xrecv.at[2, i], "tensor", t_right)
        return remote(recv_buf.at[2, m], recv_buf.at[3, m], xsend.at[2, i], xrecv.at[2, i], "tensor", t_left)

    def spread_group(i):
        ywait(i)
        xcopy(0, i).start()
        xcopy(1, i).start()

    def hand_on(i):
        xcopy(0 if i < 2 else 1, i).wait_recv()
        xcopy(2, i).start()

    def forward(first, last):
        rows = slice(first, last)
        x = xb[rows, :]
        pre_gate = dot(x, wg[...], nt)
        pre_up = dot(x, wu[...], nt)
        sig = jax.nn.sigmoid(pre_gate)
        silu = pre_gate * sig
        silu_s[rows, :] = silu
        slope_up[rows, :] = pre_up * (sig * (1.0 + pre_gate * (1.0 - sig)))
        hid_s[rows, :] = (silu * pre_up).astype(BF16)

    nt = ((1,), (1,))
    place_t[...] = place[...].T
    spread_group(0)
    opening, closing = unpack_matrices(cap, pieces + 1, n_exp)
    unpack[...] = opening.astype(BF16)
    pack[...] = closing.astype(BF16)
    spread_group(1)
    hand_on(0)
    for i in (3, 4, 5):
        loads[i].wait()
    forward(0, 2 * slots)
    spread_group(2)
    hand_on(1)
    forward(2 * slots, 4 * slots)
    spread_group(3)
    hand_on(2)
    xt[...] = xb[...].T
    hand_on(3)
    loads[6].wait()

    lane_q = iota((slots, LANES), 1) == q

    def rows_of(tt):
        return pl.ds(pl.multiple_of(tt * slots, 32), slots)

    def backward(rel, tt):
        rows = rows_of(tt)
        opened = dot(unpack[...], recv_buf[rel].reshape(n_exp * CHUNK, LANES))

        def piece(j):
            return opened[slots * j : slots * (j + 1), :]

        weight = jnp.sum(jnp.where(lane_q, piece(pieces), 0.0), axis=1, keepdims=True)
        for j in range(pieces):
            cols = slice(LANES * j, LANES * (j + 1))
            val = piece(j)
            dy[rows, cols] = val.astype(BF16)
            scaled[rows, cols] = (weight * val).astype(BF16)
        back = dot(dy[rows, :], wd[...], nt)
        prob = jnp.sum(hid_s[rows, :].astype(F32) * back, axis=1, keepdims=True)
        prob_s[rows, :] = jnp.broadcast_to(prob, (slots, 128))
        hidden_grad = weight * back
        gate_g[rows, :] = (hidden_grad * slope_up[rows, :]).astype(BF16)
        up_g[rows, :] = (hidden_grad * silu_s[rows, :]).astype(BF16)

    backward(0, t)
    for i in (2, 3):
        xcopy(0, i).wait_recv()
    backward(1, t_left)
    for i in (0, 1):
        xcopy(1, i).wait_recv()
    backward(2, t_right)
    for i in range(4):
        xcopy(2, i).wait_recv()
    backward(3, t_opp)

    def input_part(tt):
        rows = rows_of(tt)
        return dot(gate_g[rows, :], wg[...]) + dot(up_g[rows, :], wu[...])

    def put_part(ref, tt):
        ref[:, :d] = input_part(tt).astype(BF16)
        ref[:, d:] = prob_s[rows_of(tt), :].astype(BF16)

    lo, hi = pl.ds(0, half), pl.ds(half, half)
    first_right = remote(xs_opp.at[lo], xr1.at[0], rsend.at[0], rrecv.at[0], "tensor", t_right)
    first_left = remote(xs_opp.at[hi], xr1.at[1], rsend.at[1], rrecv.at[1], "tensor", t_left)
    plain_right = remote(xs_right.at[hi], xr2.at[0, hi], rsend.at[2], rrecv.at[2], "tensor", t_right)
    plain_left = remote(xs_left.at[lo], xr2.at[1, lo], rsend.at[3], rrecv.at[3], "tensor", t_left)
    added_right = remote(xs_right.at[lo], xr2.at[0, lo], rsend.at[4], rrecv.at[4], "tensor", t_right)
    added_left = remote(xs_left.at[hi], xr2.at[1, hi], rsend.at[5], rrecv.at[5], "tensor", t_left)

    put_part(xs_opp, t_opp)
    first_right.start()
    first_left.start()

    rows_z = d // n_dp
    last = n_dp - 2

    def zcopy(sub, s, src):
        return remote(
            src, zbuf.at[sub, s], zsend.at[sub, s], zrecv.at[sub, s], "dp", g_right if sub % 2 == 0 else g_left
        )

    def zrows(sub, s):
        owner = (g + 2 * n_dp - 1 - s) % n_dp if sub % 2 == 0 else (g + 1 + s) % n_dp
        return pl.ds(pl.multiple_of(owner * rows_z, 16), rows_z)

    def zfirst(sub):
        zcopy(sub, 0, dw.at[sub, zrows(sub, 0)]).start()

    def zstep(s, carry):
        for sub in range(4):
            zcopy(sub, s - 1, zbuf.at[sub, s - 1]).wait_recv()
            total = zbuf[sub, s - 1].astype(F32) + dw[sub, zrows(sub, s), :].astype(F32)
            zbuf[sub, s - 1] = total.astype(BF16)
            zcopy(sub, s, zbuf.at[sub, s - 1]).start()
        return carry

    def zsteps(first, end):
        lax.fori_loop(first, end, zstep, 0)

    dw[0] = dot(xt[...], gate_g[:, :LANES]).astype(BF16)
    zfirst(0)
    dw[1] = dot(xt[...], up_g[:, :LANES]).astype(BF16)
    zfirst(1)
    scaled_t = scaled[...].T
    dw[2] = dot(scaled_t, hid_s[:, :LANES]).astype(BF16)
    zfirst(2)
    rest = hid - LANES
    gate_up = jnp.concatenate([gate_g[:, LANES:], up_g[:, LANES:]], axis=1)
    dw[3, :, : 2 * rest] = dot(xt[...], gate_up).astype(BF16)
    dw[3, :, 2 * rest :] = jnp.concatenate(
        [dot(scaled_t, hid_s[:, LANES:]), jnp.zeros((d, LANES - 3 * rest), F32)], axis=1
    ).astype(BF16)
    zfirst(3)
    put_part(xs_right, t_right)
    plain_right.start()
    put_part(xs_left, t_left)
    plain_left.start()

    zsteps(1, 3)
    first_right.wait_recv()
    xs_right[lo, :] = (xs_right[lo, :].astype(F32) + xr1[0].astype(F32)).astype(BF16)
    added_right.start()
    first_left.wait_recv()
    xs_left[hi, :] = (xs_left[hi, :].astype(F32) + xr1[1].astype(F32)).astype(BF16)
    added_left.start()

    zsteps(3, 6)
    for copy in (plain_right, plain_left, added_right, added_left):
        copy.wait_recv()
    slot_input = input_part(t) + xr2[0, :, :d].astype(F32) + xr2[1, :, :d].astype(F32)
    slot_prob = prob_s[rows_of(t), :] + xr2[0, :, d:].astype(F32) + xr2[1, :, d:].astype(F32)
    slot_prob = jnp.where(lane_q, jnp.concatenate([slot_prob] * (LANES // 128), axis=1), 0.0)
    pile = jnp.concatenate(
        [slot_input[:, LANES * j : LANES * (j + 1)] for j in range(pieces)] + [slot_prob], axis=0
    ).astype(BF16)
    ret_send[...] = dot(pack[...], pile).astype(BF16).reshape(n_exp, CHUNK, LANES)

    def wcopy(i):
        p = partner(i)
        return remote(ret_send.at[p], ret_recv.at[q], wsend.at[p], wrecv.at[q], "expert", p)

    def wstart(i, carry):
        wcopy(i).start()
        return carry

    lax.fori_loop(0, n_exp - 1, wstart, 0)
    ret_recv[pl.ds(q, 1)] = ret_send[pl.ds(q, 1)]

    zsteps(6, 10)

    def wwait(i, carry):
        p = partner(i)
        remote(ret_send.at[p], ret_recv.at[p], wsend.at[p], wrecv.at[p], "expert", p).wait_recv()
        return carry

    lax.fori_loop(0, n_exp - 1, wwait, 0)
    tokens = dot(place_t[...], ret_recv[...].reshape(n_exp * CHUNK, LANES))
    for j in range(pieces):
        gather[0, :, LANES * j : LANES * (j + 1)] = tokens[share * j : share * (j + 1), :].astype(BF16)
    prob_pos = tokens[share * pieces :, :128]
    prob_tk = jnp.zeros((share, 128), F32)
    for k in range(top):
        val = jnp.sum(jnp.where(ids[:, k : k + 1] == name, prob_pos, 0.0), axis=1, keepdims=True)
        prob_tk = jnp.where(lane == k, val, prob_tk)
    gather[0, :, d:] = prob_tk.astype(BF16)

    low, high = pl.ds(0, share // 2), pl.ds(share // 2, share // 2)
    to_right = remote(gather.at[0], gather.at[1], gsend.at[0], grecv.at[0], "tensor", t_right)
    to_left = remote(gather.at[0], gather.at[2], gsend.at[1], grecv.at[1], "tensor", t_left)
    on_right = remote(gather.at[1, low], gather.at[3, low], gsend.at[2], grecv.at[2], "tensor", t_right)
    on_left = remote(gather.at[2, high], gather.at[3, high], gsend.at[3], grecv.at[3], "tensor", t_left)
    to_right.start()
    to_left.start()

    def put_tokens(rel, tt):
        rows = pl.ds(pl.multiple_of(tt * share, share), share)
        out_ref[rows, :] = gather[rel, :, :d]
        prob_all[rows, :] = gather[rel, :, d:].astype(F32)

    zsteps(10, 12)
    put_tokens(0, t)
    to_right.wait_recv()
    on_right.start()
    to_left.wait_recv()
    on_left.start()
    zsteps(12, last + 1)
    put_tokens(1, t_left)
    put_tokens(2, t_right)
    on_right.wait_recv()
    on_left.wait_recv()
    put_tokens(3, t_opp)

    own = []
    for sub in range(4):
        zcopy(sub, last, zbuf.at[sub, last]).wait_recv()
        own.append(zbuf[sub, last].astype(F32) + dw[sub, zrows(sub, last + 1), :].astype(F32))
    own = [jnp.concatenate([o, jnp.zeros((128 - rows_z, LANES), F32)], axis=0).T[:, :rows_z] for o in own]
    gate_out[:LANES, :] = own[0]
    gate_out[LANES:, :] = own[3][:rest]
    up_out[:LANES, :] = own[1]
    up_out[LANES:, :] = own[3][rest : 2 * rest]
    down_out[:LANES, :] = own[2]
    down_out[LANES:, :] = own[3][2 * rest : 3 * rest]
    prob_out[...] = prob_all[...].T[:top]

    def sent(i, carry):
        ycopy(i).wait_send()
        wcopy(i).wait_send()
        return carry

    lax.fori_loop(0, n_exp - 1, sent, 0)
    for kind in range(3):
        for i in range(4):
            xcopy(kind, i).wait_send()
    for copy in (first_right, first_left, plain_right, plain_left, added_right, added_left):
        copy.wait_send()
    for copy in (to_right, to_left, on_right, on_left):
        copy.wait_send()

    def zsent(s, carry):
        for sub in range(4):
            zcopy(sub, s, zbuf.at[sub, s]).wait_send()
        return carry

    lax.fori_loop(0, n_dp - 1, zsent, 0)


def shards(grad_out, expert_ids, gate_probs, saved_inputs, w_gate, w_up, w_down):
    n_dp, n_exp, n_ten = lax.axis_size("dp"), lax.axis_size("expert"), lax.axis_size("tensor")
    tok_rows, d = grad_out.shape
    cap, top, hid = saved_inputs.shape[4], expert_ids.shape[1], w_gate.shape[2]
    share = tok_rows // n_ten
    slots = n_exp * cap
    total = n_ten * slots
    wide = d + 128
    rows_z = d // n_dp
    vmem = pltpu.VMEM
    dma = pltpu.SemaphoreType.DMA
    outs = pl.pallas_call(
        lambda *refs: kernel((n_dp, n_exp, n_ten, cap, top, d, hid), *refs),
        out_shape=(
            jax.ShapeDtypeStruct((tok_rows, d), BF16),
            jax.ShapeDtypeStruct((top, tok_rows), F32),
            jax.ShapeDtypeStruct((hid, rows_z), F32),
            jax.ShapeDtypeStruct((hid, rows_z), F32),
            jax.ShapeDtypeStruct((hid, rows_z), F32),
        ),
        in_specs=[pl.BlockSpec(memory_space=pl.ANY)] * 7,
        out_specs=(pl.BlockSpec(memory_space=pltpu.VMEM),) * 5,
        scratch_shapes=[
            vmem((share, d), BF16),
            vmem((top, tok_rows), jnp.int32),
            vmem((top, tok_rows), F32),
            vmem((total, d), BF16),
            vmem((hid, d), BF16),
            vmem((hid, d), BF16),
            vmem((hid, d), BF16),
            vmem((tok_rows, 128), F32),
            vmem((tok_rows, 128), F32),
            vmem((tok_rows, 128), F32),
            vmem((n_exp * CHUNK, n_exp * CHUNK), BF16),
            vmem((n_exp * CHUNK, n_exp * CHUNK), BF16),
            vmem((n_exp, CHUNK, LANES), BF16),
            vmem((4, n_exp, CHUNK, LANES), BF16),
            vmem((n_exp * CHUNK, LANES), BF16),
            vmem((LANES, n_exp * CHUNK), BF16),
            vmem((d, total), BF16),
            vmem((total, hid), F32),
            vmem((total, hid), F32),
            vmem((total, hid), BF16),
            vmem((total, d), BF16),
            vmem((total, d), BF16),
            vmem((total, hid), BF16),
            vmem((total, hid), BF16),
            vmem((total, 128), F32),
            vmem((slots, wide), BF16),
            vmem((slots, wide), BF16),
            vmem((slots, wide), BF16),
            vmem((2, slots // 2, wide), BF16),
            vmem((2, slots, wide), BF16),
            vmem((n_exp, CHUNK, LANES), BF16),
            vmem((n_exp, CHUNK, LANES), BF16),
            vmem((4, share, wide), BF16),
            vmem((4, d, LANES), BF16),
            vmem((4, n_dp - 1, rows_z, LANES), BF16),
            dma((7,)),
            dma((n_exp,)),
            dma((n_exp,)),
            dma((3, 4)),
            dma((3, 4)),
            dma((6,)),
            dma((6,)),
            dma((n_exp,)),
            dma((n_exp,)),
            dma((4,)),
            dma((4,)),
            dma((4, n_dp - 1)),
            dma((4, n_dp - 1)),
        ],
        compiler_params=pltpu.CompilerParams(
            collective_id=0, has_side_effects=True, vmem_limit_bytes=56 * 1024 * 1024
        ),
        name="expert_backward",
    )(
        grad_out,
        expert_ids.T,
        gate_probs.T,
        saved_inputs.transpose(0, 1, 2, 4, 3, 5).reshape(total, d),
        w_gate[0].T,
        w_up[0].T,
        w_down[0].T,
    )
    return outs[0], outs[1].T, outs[2].T[None], outs[3].T[None], outs[4].T[None]


def solution(mesh):
    return jax.shard_map(
        shards,
        mesh=mesh,
        in_specs=(
            P(("dp", "expert"), None),
            P(("dp", "expert"), None),
            P(("dp", "expert"), None),
            P("dp", "expert", None, None, None, None),
            P("expert", None, "tensor"),
            P("expert", None, "tensor"),
            P("expert", None, "tensor"),
        ),
        out_specs=(
            P(("dp", "expert"), None),
            P(("dp", "expert"), None),
            P("expert", "dp", "tensor"),
            P("expert", "dp", "tensor"),
            P("expert", "dp", "tensor"),
        ),
        check_vma=False,
    )
```

time: 245 us -> 117 us (0.48)
  the two profiles are of different devices: /device:TPU:12 before, /device:TPU:16 now
where the time goes in v1:
time: 117 us
  Pallas kernels  110 us (94%)
  local copies, waits for them, and re-layouts  6.06 us (5%)
    pallas_call x1, Pallas kernels, shards(): pl.pallas_call(lambda *refs: kernel((n_dp, n_exp, n_ten, cap, top, d, hid...  110 us
    unnamed x9, local copies, waits for them, and re-layouts  6.06 us

profile of v1, /device:TPU:16, one launch (start us, length us, event | category | flops | bytes accessed | tf_op | source)
XLA Modules:
  0.0 116.9 jit_solution(4702267485181998495)
XLA Ops:
  0.6 110.2 %expert_backward.1 = (bf16[128,1792]{1,0:T(8,128)(2,1)}, f32[8,128]{1,0:T(8,128)}, f32[320,112]{1,0:T(8,128)}, f32[320,112]{1,0:T(8,128)}, f32[320,112]{1,0:T(8,128)}) custom-call(bf16[128,1792]{1,0:T(8,128)(2,1)} %refs_0_.1, s32[8,128]{1,0:T(8,128)} %bitcast.31, f32[8,128]{1,0:T(8,128)} %bitcast.32, bf16[384,1792]{1,0:T(8,128)(2,1)} %bitcast.24, ...), custom_call_target="tpu_custom_call" | custom-call | tf_op jit(solution)/shard_map/expert_backward/pallas_call | solution.py:422
  110.8 0.0 copy-start.1
  110.8 0.0 copy-start
  110.8 1.9 %copy.17 = bf16[128,1792]{1,0:T(8,128)(2,1)} copy(bf16[128,1792]{1,0:T(8,128)(2,1)} %get-tuple-element.20) | data formatting | bytes 917504
  112.7 1.3 %copy.18 = f32[128,8]{0,1:T(8,128)} copy(f32[128,8]{0,1:T(8,128)} %bitcast.33) | data formatting | bytes 8192
  114.0 1.6 %copy.19 = f32[1,112,320]{1,2,0:T(8,128)} copy(f32[1,112,320]{1,2,0:T(8,128)} %bitcast.30) | data formatting | bytes 286720
  115.6 0.0 copy-done.1
  115.6 0.7 copy.20
  116.2 0.0 copy-done
  116.2 0.7 copy.21
Async XLA Ops:
  110.8 4.7 %copy-start.1 = (f32[320,112]{1,0:T(8,128)S(1)}, f32[320,112]{1,0:T(8,128)}, u32[]{:S(2)}) copy-start(f32[320,112]{1,0:T(8,128)} %get-tuple-element.13) | copy-start | bytes 430084
  110.8 5.4 %copy-start = (f32[320,112]{1,0:T(8,128)S(1)}, f32[320,112]{1,0:T(8,128)}, u32[]{:S(2)}) copy-start(f32[320,112]{1,0:T(8,128)} %get-tuple-element.14) | copy-start | bytes 430084

commit v2 on v1

--- a/solution.py
+++ b/solution.py
@@ -38,15 +38,17 @@
     out_ref, prob_out, gate_out, up_out, down_out,
     grad_v, ids_v, probs_v, xb, wg, wu, wd, ids_s, probs_s, prob_all, unpack, pack,
     send_buf, recv_buf, place, place_t,
-    xt, slope_up, silu_s, hid_s, dy, scaled, gate_g, up_g, prob_s,
+    xt, st, slope_up, silu_s, hid_s, hid_r, gate_g, up_g, gate_up, hid_rest, prob_s, own_part,
     xs_opp, xs_left, xs_right, xr1, xr2, ret_send, ret_recv, gather,
-    dw, zbuf,
+    zfirst, zbuf,
     load_sem, ysend, yrecv, xsend, xrecv, rsend, rrecv, wsend, wrecv, gsend, grecv, zsend, zrecv,
 ):
     n_dp, n_exp, n_ten, cap, top, d, hid = sizes
     share = grad_v.shape[0]
     pieces = d // LANES
-    group = n_exp // 4
+    group = 2
+    groups = n_exp // group
+    rest = hid - LANES
     slots = n_exp * cap
     half = slots // 2
     g, q, t = lax.axis_index("dp"), lax.axis_index("expert"), lax.axis_index("tensor")
@@ -131,7 +133,10 @@
     recv_buf[0, pl.ds(q, 1)] = send_buf[pl.ds(q, 1)]
 
     mine = q // group
-    order = [mine, (mine + 1) % 4, (mine + 3) % 4, (mine + 2) % 4]
+    order = [mine]
+    for away in range(1, groups // 2):
+        order += [(mine + away) % groups, (mine + groups - away) % groups]
+    order.append((mine + groups // 2) % groups)
 
     def members(i):
         return pl.ds(order[i] * group, group)
@@ -154,7 +159,7 @@
             return remote(recv_buf.at[0, m], recv_buf.at[1, m], xsend.at[0, i], xrecv.at[0, i], "tensor", t_right)
         if kind == 1:
             return remote(recv_buf.at[0, m], recv_buf.at[2, m], xsend.at[1, i], xrecv.at[1, i], "tensor", t_left)
-        if i < 2:
+        if i % 2 == 0:
             return remote(recv_buf.at[1, m], recv_buf.at[3, m], xsend.at[2, i], xrecv.at[2, i], "tensor", t_right)
         return remote(recv_buf.at[2, m], recv_buf.at[3, m], xsend.at[2, i], xrecv.at[2, i], "tensor", t_left)
 
@@ -164,7 +169,7 @@
         xcopy(1, i).start()
 
     def hand_on(i):
-        xcopy(0 if i < 2 else 1, i).wait_recv()
+        xcopy(i % 2, i).wait_recv()
         xcopy(2, i).start()
 
     def forward(first, last):
@@ -179,26 +184,34 @@
         hid_s[rows, :] = (silu * pre_up).astype(BF16)
 
     nt = ((1,), (1,))
+    spread_group(0)
     place_t[...] = place[...].T
-    spread_group(0)
+    spread_group(1)
     opening, closing = unpack_matrices(cap, pieces + 1, n_exp)
     unpack[...] = opening.astype(BF16)
+    hand_on(0)
+    spread_group(2)
     pack[...] = closing.astype(BF16)
-    spread_group(1)
-    hand_on(0)
+    hand_on(1)
     for i in (3, 4, 5):
         loads[i].wait()
-    forward(0, 2 * slots)
-    spread_group(2)
-    hand_on(1)
-    forward(2 * slots, 4 * slots)
     spread_group(3)
     hand_on(2)
+    forward(0, 2 * slots)
+    spread_group(4)
+    hand_on(3)
+    forward(2 * slots, 4 * slots)
+    spread_group(5)
+    hand_on(4)
     xt[...] = xb[...].T
-    hand_on(3)
     loads[6].wait()
+    spread_group(6)
+    hand_on(5)
+    spread_group(7)
+    hand_on(6)
 
     lane_q = iota((slots, LANES), 1) == q
+    blank = 128 - slots
 
     def rows_of(tt):
         return pl.ds(pl.multiple_of(tt * slots, 32), slots)
@@ -211,12 +224,11 @@
             return opened[slots * j : slots * (j + 1), :]
 
         weight = jnp.sum(jnp.where(lane_q, piece(pieces), 0.0), axis=1, keepdims=True)
-        for j in range(pieces):
-            cols = slice(LANES * j, LANES * (j + 1))
-            val = piece(j)
-            dy[rows, cols] = val.astype(BF16)
-            scaled[rows, cols] = (weight * val).astype(BF16)
-        back = dot(dy[rows, :], wd[...], nt)
+        dy = jnp.concatenate([piece(j) for j in range(pieces)], axis=1)
+        at = slice(128 * rel, 128 * (rel + 1))
+        st[:, at] = jnp.concatenate([(weight * dy).astype(BF16), jnp.zeros((blank, d), BF16)], axis=0).T
+        hid_r[at, :] = jnp.concatenate([hid_s[rows, :], jnp.zeros((blank, hid), BF16)], axis=0)
+        back = dot(dy.astype(BF16), wd[...], nt)
         prob = jnp.sum(hid_s[rows, :].astype(F32) * back, axis=1, keepdims=True)
         prob_s[rows, :] = jnp.broadcast_to(prob, (slots, 128))
         hidden_grad = weight * back
@@ -224,15 +236,18 @@
         up_g[rows, :] = (hidden_grad * silu_s[rows, :]).astype(BF16)
 
     backward(0, t)
-    for i in (2, 3):
+    hand_on(7)
+    for i in range(1, groups, 2):
         xcopy(0, i).wait_recv()
     backward(1, t_left)
-    for i in (0, 1):
+    for i in range(0, groups, 2):
         xcopy(1, i).wait_recv()
     backward(2, t_right)
-    for i in range(4):
+    for i in range(groups):
         xcopy(2, i).wait_recv()
     backward(3, t_opp)
+    gate_up[...] = jnp.concatenate([gate_g[:, LANES:], up_g[:, LANES:]], axis=1)
+    hid_rest[...] = jnp.concatenate([hid_r[:, LANES:], jnp.zeros((4 * 128, 128 - rest), BF16)], axis=1)
 
     def input_part(tt):
         rows = rows_of(tt)
@@ -250,67 +265,75 @@
     added_right = remote(xs_right.at[lo], xr2.at[0, lo], rsend.at[4], rrecv.at[4], "tensor", t_right)
     added_left = remote(xs_left.at[hi], xr2.at[1, hi], rsend.at[5], rrecv.at[5], "tensor", t_left)
 
+    rows_z = d // n_dp
+    hops = n_dp // 2
+
+    def zcopy(way, sub, s, src):
+        return remote(
+            src, zbuf.at[way, sub, s], zsend.at[way, sub, s], zrecv.at[way, sub, s], "dp", g_left if way else g_right
+        )
+
+    def zrows(way, s):
+        owner = (g + hops + s) % n_dp if way else (g + n_dp + hops - s) % n_dp
+        return pl.ds(pl.multiple_of(owner * rows_z, 16), rows_z)
+
+    def term(sub, chunks):
+        def left(ref):
+            return jnp.concatenate([ref[rows, :] for rows in chunks], axis=0)
+
+        if sub == 0:
+            return dot(left(xt), gate_g[:, :LANES])
+        if sub == 1:
+            return dot(left(xt), up_g[:, :LANES])
+        if sub == 2:
+            return dot(left(st), hid_r[:, :LANES])
+        return jnp.concatenate([dot(left(xt), gate_up[...]), dot(left(st), hid_rest[...])], axis=1)
+
+    def zpiece(s, sub, got):
+        terms = term(sub, [zrows(0, s), zrows(1, s)])
+        for way in range(2):
+            total = terms[rows_z * way : rows_z * (way + 1), :]
+            slot = zbuf.at[way, sub, s - 1]
+            if got[way]:
+                zcopy(way, sub, s - 1, slot).wait_recv()
+                total = total + slot[...].astype(F32)
+            slot[...] = total.astype(BF16)
+            zcopy(way, sub, s, slot).start()
+
+    def zsteps(first, end):
+        def step(s, carry):
+            for sub in range(4):
+                zpiece(s, sub, (True, True))
+            return carry
+
+        lax.fori_loop(first, end, step, 0)
+
+    for sub in (0, 2, 1, 3):
+        zfirst[sub] = term(sub, [zrows(0, 0)]).astype(BF16)
+        zcopy(sub // 2, sub, 0, zfirst.at[sub]).start()
     put_part(xs_opp, t_opp)
     first_right.start()
     first_left.start()
 
-    rows_z = d // n_dp
-    last = n_dp - 2
-
-    def zcopy(sub, s, src):
-        return remote(
-            src, zbuf.at[sub, s], zsend.at[sub, s], zrecv.at[sub, s], "dp", g_right if sub % 2 == 0 else g_left
-        )
-
-    def zrows(sub, s):
-        owner = (g + 2 * n_dp - 1 - s) % n_dp if sub % 2 == 0 else (g + 1 + s) % n_dp
-        return pl.ds(pl.multiple_of(owner * rows_z, 16), rows_z)
-
-    def zfirst(sub):
-        zcopy(sub, 0, dw.at[sub, zrows(sub, 0)]).start()
-
-    def zstep(s, carry):
-        for sub in range(4):
-            zcopy(sub, s - 1, zbuf.at[sub, s - 1]).wait_recv()
-            total = zbuf[sub, s - 1].astype(F32) + dw[sub, zrows(sub, s), :].astype(F32)
-            zbuf[sub, s - 1] = total.astype(BF16)
-            zcopy(sub, s, zbuf.at[sub, s - 1]).start()
-        return carry
-
-    def zsteps(first, end):
-        lax.fori_loop(first, end, zstep, 0)
-
-    dw[0] = dot(xt[...], gate_g[:, :LANES]).astype(BF16)
-    zfirst(0)
-    dw[1] = dot(xt[...], up_g[:, :LANES]).astype(BF16)
-    zfirst(1)
-    scaled_t = scaled[...].T
-    dw[2] = dot(scaled_t, hid_s[:, :LANES]).astype(BF16)
-    zfirst(2)
-    rest = hid - LANES
-    gate_up = jnp.concatenate([gate_g[:, LANES:], up_g[:, LANES:]], axis=1)
-    dw[3, :, : 2 * rest] = dot(xt[...], gate_up).astype(BF16)
-    dw[3, :, 2 * rest :] = jnp.concatenate(
-        [dot(scaled_t, hid_s[:, LANES:]), jnp.zeros((d, LANES - 3 * rest), F32)], axis=1
-    ).astype(BF16)
-    zfirst(3)
+    for sub in range(4):
+        zpiece(1, sub, (sub < 2, sub >= 2))
     put_part(xs_right, t_right)
     plain_right.start()
     put_part(xs_left, t_left)
     plain_left.start()
-
-    zsteps(1, 3)
+    zsteps(2, 3)
     first_right.wait_recv()
     xs_right[lo, :] = (xs_right[lo, :].astype(F32) + xr1[0].astype(F32)).astype(BF16)
     added_right.start()
     first_left.wait_recv()
     xs_left[hi, :] = (xs_left[hi, :].astype(F32) + xr1[1].astype(F32)).astype(BF16)
     added_left.start()
-
-    zsteps(3, 6)
+    own_part[...] = input_part(t)
+
+    zsteps(3, 4)
     for copy in (plain_right, plain_left, added_right, added_left):
         copy.wait_recv()
-    slot_input = input_part(t) + xr2[0, :, :d].astype(F32) + xr2[1, :, :d].astype(F32)
+    slot_input = own_part[...] + xr2[0, :, :d].astype(F32) + xr2[1, :, :d].astype(F32)
     slot_prob = prob_s[rows_of(t), :] + xr2[0, :, d:].astype(F32) + xr2[1, :, d:].astype(F32)
     slot_prob = jnp.where(lane_q, jnp.concatenate([slot_prob] * (LANES // 128), axis=1), 0.0)
     pile = jnp.concatenate(
@@ -329,7 +352,7 @@
     lax.fori_loop(0, n_exp - 1, wstart, 0)
     ret_recv[pl.ds(q, 1)] = ret_send[pl.ds(q, 1)]
 
-    zsteps(6, 10)
+    zsteps(4, 6)
 
     def wwait(i, carry):
         p = partner(i)
@@ -360,13 +383,13 @@
         out_ref[rows, :] = gather[rel, :, :d]
         prob_all[rows, :] = gather[rel, :, d:].astype(F32)
 
-    zsteps(10, 12)
     put_tokens(0, t)
+    zsteps(6, 7)
     to_right.wait_recv()
     on_right.start()
     to_left.wait_recv()
     on_left.start()
-    zsteps(12, last + 1)
+    zsteps(7, hops)
     put_tokens(1, t_left)
     put_tokens(2, t_right)
     on_right.wait_recv()
@@ -375,8 +398,11 @@
 
     own = []
     for sub in range(4):
-        zcopy(sub, last, zbuf.at[sub, last]).wait_recv()
-        own.append(zbuf[sub, last].astype(F32) + dw[sub, zrows(sub, last + 1), :].astype(F32))
+        total = term(sub, [zrows(0, hops)])
+        for way in range(2):
+            zcopy(way, sub, hops - 1, zbuf.at[way, sub, hops - 1]).wait_recv()
+            total = total + zbuf[way, sub, hops - 1].astype(F32)
+        own.append(total)
     own = [jnp.concatenate([o, jnp.zeros((128 - rows_z, LANES), F32)], axis=0).T[:, :rows_z] for o in own]
     gate_out[:LANES, :] = own[0]
     gate_out[LANES:, :] = own[3][:rest]
@@ -393,19 +419,28 @@
 
     lax.fori_loop(0, n_exp - 1, sent, 0)
     for kind in range(3):
-        for i in range(4):
+        for i in range(groups):
             xcopy(kind, i).wait_send()
     for copy in (first_right, first_left, plain_right, plain_left, added_right, added_left):
         copy.wait_send()
     for copy in (to_right, to_left, on_right, on_left):
         copy.wait_send()
 
+    for sub in range(4):
+        zcopy(sub // 2, sub, 0, zfirst.at[sub]).wait_send()
+
     def zsent(s, carry):
-        for sub in range(4):
-            zcopy(sub, s, zbuf.at[sub, s]).wait_send()
+        for way in range(2):
+            for sub in range(4):
+                zcopy(way, sub, s, zbuf.at[way, sub, s]).wait_send()
         return carry
 
-    lax.fori_loop(0, n_dp - 1, zsent, 0)
+    lax.fori_loop(1, hops, zsent, 0)
+
+
+def finish(*refs):
+    for src, dst in zip(refs[:5], refs[5:]):
+        dst[...] = src[...]
 
 
 def shards(grad_out, expert_ids, gate_probs, saved_inputs, w_gate, w_up, w_down):
@@ -419,15 +454,16 @@
     rows_z = d // n_dp
     vmem = pltpu.VMEM
     dma = pltpu.SemaphoreType.DMA
+    shapes = (
+        jax.ShapeDtypeStruct((tok_rows, d), BF16),
+        jax.ShapeDtypeStruct((top, tok_rows), F32),
+        jax.ShapeDtypeStruct((hid, rows_z), F32),
+        jax.ShapeDtypeStruct((hid, rows_z), F32),
+        jax.ShapeDtypeStruct((hid, rows_z), F32),
+    )
     outs = pl.pallas_call(
         lambda *refs: kernel((n_dp, n_exp, n_ten, cap, top, d, hid), *refs),
-        out_shape=(
-            jax.ShapeDtypeStruct((tok_rows, d), BF16),
-            jax.ShapeDtypeStruct((top, tok_rows), F32),
-            jax.ShapeDtypeStruct((hid, rows_z), F32),
-            jax.ShapeDtypeStruct((hid, rows_z), F32),
-            jax.ShapeDtypeStruct((hid, rows_z), F32),
-        ),
+        out_shape=shapes,
         in_specs=[pl.BlockSpec(memory_space=pl.ANY)] * 7,
         out_specs=(pl.BlockSpec(memory_space=pltpu.VMEM),) * 5,
         scratch_shapes=[
@@ -448,14 +484,17 @@
             vmem((n_exp * CHUNK, LANES), BF16),
             vmem((LANES, n_exp * CHUNK), BF16),
             vmem((d, total), BF16),
+            vmem((d, 4 * 128), BF16),
             vmem((total, hid), F32),
             vmem((total, hid), F32),
             vmem((total, hid), BF16),
-            vmem((total, d), BF16),
-            vmem((total, d), BF16),
+            vmem((4 * 128, hid), BF16),
             vmem((total, hid), BF16),
             vmem((total, hid), BF16),
+            vmem((total, 128), BF16),
+            vmem((4 * 128, 128), BF16),
             vmem((total, 128), F32),
+            vmem((slots, d), F32),
             vmem((slots, wide), BF16),
             vmem((slots, wide), BF16),
             vmem((slots, wide), BF16),
@@ -464,21 +503,21 @@
             vmem((n_exp, CHUNK, LANES), BF16),
             vmem((n_exp, CHUNK, LANES), BF16),
             vmem((4, share, wide), BF16),
-            vmem((4, d, LANES), BF16),
-            vmem((4, n_dp - 1, rows_z, LANES), BF16),
+            vmem((4, rows_z, LANES), BF16),
+            vmem((2, 4, n_dp // 2, rows_z, LANES), BF16),
             dma((7,)),
             dma((n_exp,)),
             dma((n_exp,)),
-            dma((3, 4)),
-            dma((3, 4)),
+            dma((3, n_exp // 2)),
+            dma((3, n_exp // 2)),
             dma((6,)),
             dma((6,)),
             dma((n_exp,)),
             dma((n_exp,)),
             dma((4,)),
             dma((4,)),
-            dma((4, n_dp - 1)),
-            dma((4, n_dp - 1)),
+            dma((2, 4, n_dp // 2)),
+            dma((2, 4, n_dp // 2)),
         ],
         compiler_params=pltpu.CompilerParams(
             collective_id=0, has_side_effects=True, vmem_limit_bytes=56 * 1024 * 1024
@@ -493,6 +532,13 @@
         w_up[0].T,
         w_down[0].T,
     )
+    outs = pl.pallas_call(
+        finish,
+        out_shape=shapes,
+        in_specs=[pl.BlockSpec(memory_space=pltpu.VMEM)] * 5,
+        out_specs=(pl.BlockSpec(memory_space=pltpu.VMEM),) * 5,
+        name="write_results",
+    )(*outs)
     return outs[0], outs[1].T, outs[2].T[None], outs[3].T[None], outs[4].T[None]
 
 

time: 117 us -> 93.4 us (0.80)
  the two profiles are of different devices: /device:TPU:16 before, /device:TPU:1 now
where the time goes in v2:
time: 93.4 us; the launch traced here: 93.2 us
  Pallas kernels  92.6 us (99%)
    pallas_call x1, Pallas kernels, shards(): pl.pallas_call(lambda *refs: kernel((n_dp, n_exp, n_ten, cap, top, d, hid...  90.4 us
    pallas_call x1, Pallas kernels, shards(): pl.pallas_call(finish, out_shape=shapes, in_specs=[pl.BlockSpec(memory_sp...  2.13 us

profile of v2, /device:TPU:1, one launch (start us, length us, event | category | flops | bytes accessed | tf_op | source)
XLA Modules:
  0.0 93.2 jit_solution(4196275697681810166)
XLA Ops:
  0.6 90.4 %expert_backward.1 = (bf16[128,1792]{1,0:T(8,128)(2,1)}, f32[8,128]{1,0:T(8,128)}, f32[320,112]{1,0:T(8,128)}, f32[320,112]{1,0:T(8,128)}, f32[320,112]{1,0:T(8,128)}) custom-call(bf16[128,1792]{1,0:T(8,128)(2,1)} %refs_0_.1, s32[8,128]{1,0:T(8,128)} %bitcast.28, f32[8,128]{1,0:T(8,128)} %bitcast.29, bf16[384,1792]{1,0:T(8,128)(2,1)} %bitcast.24, ...), custom_call_target="tpu_custom_call" | custom-call | tf_op jit(solution)/shard_map/expert_backward/pallas_call | solution.py:464
  91.1 2.1 %write_results.1 = (bf16[128,1792]{1,0:T(8,128)(2,1)}, f32[8,128]{1,0:T(8,128)}, f32[320,112]{1,0:T(8,128)}, f32[320,112]{1,0:T(8,128)}, f32[320,112]{1,0:T(8,128)}) custom-call(bf16[128,1792]{1,0:T(8,128)(2,1)} %get-tuple-element.15.refs_0_, f32[8,128]{1,0:T(8,128)} %get-tuple-element.16.refs_1_, f32[320,112]{1,0:T(8,128)} %get-tuple-element.17.refs_2_, ...), custom_call_target="tpu_custom_call" | custom-call | tf_op jit(solution)/shard_map/write_results/pallas_call | solution.py:535

commit v3 on v2

--- a/solution.py
+++ b/solution.py
@@ -37,14 +37,14 @@
     grad_hbm, ids_hbm, probs_hbm, x_hbm, wg_hbm, wu_hbm, wd_hbm,
     out_ref, prob_out, gate_out, up_out, down_out,
     grad_v, ids_v, probs_v, xb, wg, wu, wd, ids_s, probs_s, prob_all, unpack, pack,
-    send_buf, recv_buf, place, place_t,
+    send_buf, opp_buf, recv_buf, place_t,
     xt, st, slope_up, silu_s, hid_s, hid_r, gate_g, up_g, gate_up, hid_rest, prob_s, own_part,
     xs_opp, xs_left, xs_right, xr1, xr2, ret_send, ret_recv, gather,
-    zfirst, zbuf,
+    zfirst, zfirst_r, zbuf, zrest,
     load_sem, ysend, yrecv, xsend, xrecv, rsend, rrecv, wsend, wrecv, gsend, grecv, zsend, zrecv,
 ):
     n_dp, n_exp, n_ten, cap, top, d, hid = sizes
-    share = grad_v.shape[0]
+    share = grad_v.shape[1]
     pieces = d // LANES
     group = 2
     groups = n_exp // group
@@ -61,15 +61,18 @@
             device_id={axis: where}, device_id_type=MESH,
         )
 
-    tok = pl.ds(pl.multiple_of(t * share, share), share)
+    def tokens_of(tt):
+        return pl.ds(pl.multiple_of(tt * share, share), share)
+
     loads = [
         pltpu.make_async_copy(ids_hbm, ids_v, load_sem.at[0]),
         pltpu.make_async_copy(probs_hbm, probs_v, load_sem.at[1]),
-        pltpu.make_async_copy(grad_hbm.at[tok], grad_v, load_sem.at[2]),
+        pltpu.make_async_copy(grad_hbm.at[tokens_of(t)], grad_v.at[0], load_sem.at[2]),
         pltpu.make_async_copy(x_hbm, xb, load_sem.at[3]),
         pltpu.make_async_copy(wg_hbm, wg, load_sem.at[4]),
         pltpu.make_async_copy(wu_hbm, wu, load_sem.at[5]),
         pltpu.make_async_copy(wd_hbm, wd, load_sem.at[6]),
+        pltpu.make_async_copy(grad_hbm.at[tokens_of(t_opp)], grad_v.at[1], load_sem.at[7]),
     ]
     for load in loads:
         load.start()
@@ -85,52 +88,41 @@
 
     loads[0].wait()
     loads[1].wait()
-    tokens_all = ids_s.shape[0]
-    fill = jnp.zeros((128 - top, tokens_all), F32)
+    fill = jnp.zeros((128 - top, ids_s.shape[0]), F32)
     ids_s[...] = jnp.concatenate([ids_v[...].astype(F32), fill], axis=0).T
     probs_s[...] = jnp.concatenate([probs_v[...], fill], axis=0).T
-    ids = ids_s[tok, :]
-    probs = probs_s[tok, :]
     lane = iota((share, 128), 1)
     name = (lane * EXP_DEV).astype(F32)
-    routed = jnp.zeros((share, 128), F32)
-    prob_tok = jnp.zeros((share, 128), F32)
-    for k in range(top):
-        hit = ids[:, k : k + 1] == name
-        routed = routed + jnp.where(hit, 1.0, 0.0)
-        prob_tok = prob_tok + jnp.where(hit, probs[:, k : k + 1], 0.0)
     lower = jnp.where(iota((share, share), 1) < iota((share, share), 0), 1.0, 0.0).astype(BF16)
-    rank = dot(lower, routed.astype(BF16))
-    code = jnp.where(routed > 0.0, rank, -128.0).astype(BF16)
     spread = ((iota((share, LANES), 1) % share) == iota((share, LANES), 0)).astype(BF16)
-    code_x = dot(code, spread, ((0,), (0,)))
     rule = (iota((CHUNK, LANES), 0) - cap * (iota((CHUNK, LANES), 1) // share)).astype(F32)
-    for p in range(n_exp):
-        place[CHUNK * p : CHUNK * (p + 1), :] = jnp.where(code_x[p : p + 1, :] == rule, 1.0, 0.0).astype(BF16)
+
+    def packed(tt, grad):
+        ids = ids_s[tokens_of(tt), :]
+        probs = probs_s[tokens_of(tt), :]
+        routed = jnp.zeros((share, 128), F32)
+        prob_tok = jnp.zeros((share, 128), F32)
+        for k in range(top):
+            hit = ids[:, k : k + 1] == name
+            routed = routed + jnp.where(hit, 1.0, 0.0)
+            prob_tok = prob_tok + jnp.where(hit, probs[:, k : k + 1], 0.0)
+        rank = dot(lower, routed.astype(BF16))
+        code = jnp.where(routed > 0.0, rank, -128.0).astype(BF16)
+        code_x = dot(code, spread, ((0,), (0,)))
+        place = jnp.concatenate(
+            [jnp.where(code_x[p : p + 1, :] == rule, 1.0, 0.0).astype(BF16) for p in range(n_exp)], axis=0
+        )
+        stacked = jnp.concatenate(
+            [grad[:, LANES * j : LANES * (j + 1)] for j in range(pieces)]
+            + [jnp.concatenate([prob_tok, jnp.zeros((share, LANES - 128), F32)], axis=1).astype(BF16)],
+            axis=0,
+        )
+        return place, dot(place, stacked).astype(BF16).reshape(n_exp, CHUNK, LANES)
+
     loads[2].wait()
-    grad = grad_v[...]
-    stacked = jnp.concatenate(
-        [grad[:, LANES * j : LANES * (j + 1)] for j in range(pieces)]
-        + [jnp.concatenate([prob_tok, jnp.zeros((share, LANES - 128), F32)], axis=1).astype(BF16)],
-        axis=0,
-    )
-    send_buf[...] = dot(place[...], stacked).astype(BF16).reshape(n_exp, CHUNK, LANES)
+    place, chunks = packed(t, grad_v[0])
+    send_buf[...] = chunks
     pl.semaphore_wait(barrier, n_exp + 3)
-
-    def partner(i):
-        step = i // 2 + 1
-        return (q + (i % 2) * (n_exp - 2 * step) + step) % n_exp
-
-    def ycopy(i):
-        p = partner(i)
-        return remote(send_buf.at[p], recv_buf.at[0, q], ysend.at[p], yrecv.at[q], "expert", p)
-
-    def ystart(i, carry):
-        ycopy(i).start()
-        return carry
-
-    lax.fori_loop(0, n_exp - 1, ystart, 0)
-    recv_buf[0, pl.ds(q, 1)] = send_buf[pl.ds(q, 1)]
 
     mine = q // group
     order = [mine]
@@ -138,39 +130,64 @@
         order += [(mine + away) % groups, (mine + groups - away) % groups]
     order.append((mine + groups // 2) % groups)
 
+    def peers(i):
+        if i == 0:
+            return [order[0] * group + 1 - q % group]
+        return [order[i] * group + m for m in range(group)]
+
+    def at_distance(away):
+        return [i for i in range(groups) if (i + 1) // 2 == away]
+
+    def ycopy(kind, p):
+        src = opp_buf if kind else send_buf
+        return remote(src.at[p], recv_buf.at[3 * kind, q], ysend.at[kind, p], yrecv.at[kind, q], "expert", p)
+
+    def ystart(kind, away):
+        for i in at_distance(away):
+            for p in peers(i):
+                ycopy(kind, p).start()
+
+    def yleft(kind, away):
+        for i in at_distance(away):
+            for p in peers(i):
+                ycopy(kind, p).wait_send()
+
+    def ywait(kind, i):
+        for p in peers(i):
+            remote(
+                send_buf.at[p], recv_buf.at[3 * kind, p], ysend.at[kind, p], yrecv.at[kind, p], "expert", p
+            ).wait_recv()
+
+    for away in range(3):
+        ystart(0, away)
+    recv_buf[0, pl.ds(q, 1)] = send_buf[pl.ds(q, 1)]
+
     def members(i):
         return pl.ds(order[i] * group, group)
 
-    def ywait(i):
-        def one(m, carry):
-            src = order[i] * group + m
-
-            @pl.when(src != q)
-            def _():
-                remote(send_buf.at[src], recv_buf.at[0, src], ysend.at[src], yrecv.at[src], "expert", src).wait_recv()
-
-            return carry
-
-        lax.fori_loop(0, group, one, 0)
-
     def xcopy(kind, i):
         m = members(i)
-        if kind == 0:
-            return remote(recv_buf.at[0, m], recv_buf.at[1, m], xsend.at[0, i], xrecv.at[0, i], "tensor", t_right)
-        if kind == 1:
-            return remote(recv_buf.at[0, m], recv_buf.at[2, m], xsend.at[1, i], xrecv.at[1, i], "tensor", t_left)
-        if i % 2 == 0:
-            return remote(recv_buf.at[1, m], recv_buf.at[3, m], xsend.at[2, i], xrecv.at[2, i], "tensor", t_right)
-        return remote(recv_buf.at[2, m], recv_buf.at[3, m], xsend.at[2, i], xrecv.at[2, i], "tensor", t_left)
+        return remote(
+            recv_buf.at[0, m], recv_buf.at[1 + kind, m], xsend.at[kind, i], xrecv.at[kind, i],
+            "tensor", t_left if kind else t_right,
+        )
 
     def spread_group(i):
-        ywait(i)
+        ywait(0, i)
         xcopy(0, i).start()
         xcopy(1, i).start()
 
+    def hand(i):
+        left = i % 2
+        m = [members(6), members(5), pl.ds(order[7] * group, 1), pl.ds(order[7] * group + 1, 1)][i]
+        return remote(
+            recv_buf.at[1 + left, m], recv_buf.at[3, m], xsend.at[2, i], xrecv.at[2, i],
+            "tensor", t_left if left else t_right,
+        )
+
     def hand_on(i):
-        xcopy(i % 2, i).wait_recv()
-        xcopy(2, i).start()
+        xcopy(i % 2, [6, 5, 7, 7][i]).wait_recv()
+        hand(i).start()
 
     def forward(first, last):
         rows = slice(first, last)
@@ -185,30 +202,36 @@
 
     nt = ((1,), (1,))
     spread_group(0)
-    place_t[...] = place[...].T
+    place_t[...] = place.T
+    yleft(0, 1)
+    ystart(0, 3)
     spread_group(1)
+    spread_group(2)
+    yleft(0, 2)
+    ystart(0, 4)
+    loads[7].wait()
+    opp_buf[...] = packed(t_opp, grad_v[1])[1]
+    ystart(1, 0)
+    recv_buf[3, pl.ds(q, 1)] = opp_buf[pl.ds(q, 1)]
+    spread_group(3)
+    spread_group(4)
+    yleft(0, 3)
+    ystart(1, 1)
+    ystart(1, 2)
+    for i in (3, 4, 5):
+        loads[i].wait()
+    forward(0, 2 * slots)
     opening, closing = unpack_matrices(cap, pieces + 1, n_exp)
     unpack[...] = opening.astype(BF16)
+    spread_group(5)
+    spread_group(6)
+    forward(2 * slots, 4 * slots)
+    spread_group(7)
     hand_on(0)
-    spread_group(2)
+    hand_on(1)
     pack[...] = closing.astype(BF16)
-    hand_on(1)
-    for i in (3, 4, 5):
-        loads[i].wait()
-    spread_group(3)
-    hand_on(2)
-    forward(0, 2 * slots)
-    spread_group(4)
-    hand_on(3)
-    forward(2 * slots, 4 * slots)
-    spread_group(5)
-    hand_on(4)
     xt[...] = xb[...].T
     loads[6].wait()
-    spread_group(6)
-    hand_on(5)
-    spread_group(7)
-    hand_on(6)
 
     lane_q = iota((slots, LANES), 1) == q
     blank = 128 - slots
@@ -236,18 +259,21 @@
         up_g[rows, :] = (hidden_grad * silu_s[rows, :]).astype(BF16)
 
     backward(0, t)
-    hand_on(7)
-    for i in range(1, groups, 2):
+    hand_on(2)
+    hand_on(3)
+    for i in range(6):
         xcopy(0, i).wait_recv()
     backward(1, t_left)
-    for i in range(0, groups, 2):
+    for i in (0, 1, 2, 3, 4, 6):
         xcopy(1, i).wait_recv()
     backward(2, t_right)
-    for i in range(groups):
-        xcopy(2, i).wait_recv()
+    for i in range(5):
+        ywait(1, i)
+    for i in range(4):
+        hand(i).wait_recv()
     backward(3, t_opp)
     gate_up[...] = jnp.concatenate([gate_g[:, LANES:], up_g[:, LANES:]], axis=1)
-    hid_rest[...] = jnp.concatenate([hid_r[:, LANES:], jnp.zeros((4 * 128, 128 - rest), BF16)], axis=1)
+    hid_rest[...] = jnp.concatenate([hid_r[:, LANES:], hid_r[:, LANES:]], axis=1)
 
     def input_part(tt):
         rows = rows_of(tt)
@@ -268,9 +294,18 @@
     rows_z = d // n_dp
     hops = n_dp // 2
 
+    fold = rows_z // 2
+    first_lanes = iota((fold, 128), 1) < rest
+
+    def zslot(way, sub, s):
+        return zrest.at[way, s] if sub == 3 else zbuf.at[way, sub, s]
+
+    def zstart(sub):
+        return zfirst_r if sub == 3 else zfirst.at[sub]
+
     def zcopy(way, sub, s, src):
         return remote(
-            src, zbuf.at[way, sub, s], zsend.at[way, sub, s], zrecv.at[way, sub, s], "dp", g_left if way else g_right
+            src, zslot(way, sub, s), zsend.at[way, sub, s], zrecv.at[way, sub, s], "dp", g_left if way else g_right
         )
 
     def zrows(way, s):
@@ -281,19 +316,24 @@
         def left(ref):
             return jnp.concatenate([ref[rows, :] for rows in chunks], axis=0)
 
-        if sub == 0:
-            return dot(left(xt), gate_g[:, :LANES])
-        if sub == 1:
-            return dot(left(xt), up_g[:, :LANES])
-        if sub == 2:
-            return dot(left(st), hid_r[:, :LANES])
-        return jnp.concatenate([dot(left(xt), gate_up[...]), dot(left(st), hid_rest[...])], axis=1)
+        if sub < 3:
+            right = (gate_g, up_g, hid_r)[sub]
+            both = dot(left(st if sub == 2 else xt), right[:, :LANES])
+            return [both[rows_z * i : rows_z * (i + 1), :] for i in range(len(chunks))]
+        wide_part, narrow = dot(left(xt), gate_up[...]), dot(left(st), hid_rest[...])
+        parts = []
+        for i in range(len(chunks)):
+            at = rows_z * i
+            folded = jnp.where(first_lanes, narrow[at : at + fold, :], narrow[at + fold : at + rows_z, :])
+            pad = jnp.zeros((zfirst_r.shape[0] - rows_z - fold, 128), F32)
+            parts.append(jnp.concatenate([wide_part[at : at + rows_z, :], folded, pad], axis=0))
+        return parts
 
     def zpiece(s, sub, got):
         terms = term(sub, [zrows(0, s), zrows(1, s)])
         for way in range(2):
-            total = terms[rows_z * way : rows_z * (way + 1), :]
-            slot = zbuf.at[way, sub, s - 1]
+            total = terms[way]
+            slot = zslot(way, sub, s - 1)
             if got[way]:
                 zcopy(way, sub, s - 1, slot).wait_recv()
                 total = total + slot[...].astype(F32)
@@ -309,8 +349,8 @@
         lax.fori_loop(first, end, step, 0)
 
     for sub in (0, 2, 1, 3):
-        zfirst[sub] = term(sub, [zrows(0, 0)]).astype(BF16)
-        zcopy(sub // 2, sub, 0, zfirst.at[sub]).start()
+        zstart(sub)[...] = term(sub, [zrows(0, 0)])[0].astype(BF16)
+        zcopy(sub // 2, sub, 0, zstart(sub)).start()
     put_part(xs_opp, t_opp)
     first_right.start()
     first_left.start()
@@ -341,6 +381,10 @@
     ).astype(BF16)
     ret_send[...] = dot(pack[...], pile).astype(BF16).reshape(n_exp, CHUNK, LANES)
 
+    def partner(i):
+        step = i // 2 + 1
+        return (q + (i % 2) * (n_exp - 2 * step) + step) % n_exp
+
     def wcopy(i):
         p = partner(i)
         return remote(ret_send.at[p], ret_recv.at[q], wsend.at[p], wrecv.at[q], "expert", p)
@@ -365,6 +409,7 @@
         gather[0, :, LANES * j : LANES * (j + 1)] = tokens[share * j : share * (j + 1), :].astype(BF16)
     prob_pos = tokens[share * pieces :, :128]
     prob_tk = jnp.zeros((share, 128), F32)
+    ids = ids_s[tokens_of(t), :]
     for k in range(top):
         val = jnp.sum(jnp.where(ids[:, k : k + 1] == name, prob_pos, 0.0), axis=1, keepdims=True)
         prob_tk = jnp.where(lane == k, val, prob_tk)
@@ -398,41 +443,49 @@
 
     own = []
     for sub in range(4):
-        total = term(sub, [zrows(0, hops)])
+        total = term(sub, [zrows(0, hops)])[0]
         for way in range(2):
-            zcopy(way, sub, hops - 1, zbuf.at[way, sub, hops - 1]).wait_recv()
-            total = total + zbuf[way, sub, hops - 1].astype(F32)
+            slot = zslot(way, sub, hops - 1)
+            zcopy(way, sub, hops - 1, slot).wait_recv()
+            total = total + slot[...].astype(F32)
         own.append(total)
-    own = [jnp.concatenate([o, jnp.zeros((128 - rows_z, LANES), F32)], axis=0).T[:, :rows_z] for o in own]
+    folded = own[3][rows_z : rows_z + fold, :]
+    own[3:] = [own[3][:rows_z, :], jnp.concatenate([folded, pltpu.roll(folded, 128 - rest, 1)], axis=0)]
+    own = [jnp.concatenate([o, jnp.zeros((128 - rows_z, o.shape[1]), F32)], axis=0).T[:, :rows_z] for o in own]
     gate_out[:LANES, :] = own[0]
     gate_out[LANES:, :] = own[3][:rest]
     up_out[:LANES, :] = own[1]
     up_out[LANES:, :] = own[3][rest : 2 * rest]
     down_out[:LANES, :] = own[2]
-    down_out[LANES:, :] = own[3][2 * rest : 3 * rest]
+    down_out[LANES:, :] = own[4][:rest]
     prob_out[...] = prob_all[...].T[:top]
 
     def sent(i, carry):
-        ycopy(i).wait_send()
         wcopy(i).wait_send()
         return carry
 
     lax.fori_loop(0, n_exp - 1, sent, 0)
-    for kind in range(3):
-        for i in range(groups):
-            xcopy(kind, i).wait_send()
+    for away in (0, 4):
+        yleft(0, away)
+    for away in range(3):
+        yleft(1, away)
+    for i in range(groups):
+        xcopy(0, i).wait_send()
+        xcopy(1, i).wait_send()
+    for i in range(4):
+        hand(i).wait_send()
     for copy in (first_right, first_left, plain_right, plain_left, added_right, added_left):
         copy.wait_send()
     for copy in (to_right, to_left, on_right, on_left):
         copy.wait_send()
 
     for sub in range(4):
-        zcopy(sub // 2, sub, 0, zfirst.at[sub]).wait_send()
+        zcopy(sub // 2, sub, 0, zstart(sub)).wait_send()
 
     def zsent(s, carry):
         for way in range(2):
             for sub in range(4):
-                zcopy(way, sub, s, zbuf.at[way, sub, s]).wait_send()
+                zcopy(way, sub, s, zslot(way, sub, s)).wait_send()
         return carry
 
     lax.fori_loop(1, hops, zsent, 0)
@@ -452,6 +505,7 @@
     total = n_ten * slots
     wide = d + 128
     rows_z = d // n_dp
+    rest_rows = rows_z + -(-rows_z // 2 // 16) * 16
     vmem = pltpu.VMEM
     dma = pltpu.SemaphoreType.DMA
     shapes = (
@@ -467,7 +521,7 @@
         in_specs=[pl.BlockSpec(memory_space=pl.ANY)] * 7,
         out_specs=(pl.BlockSpec(memory_space=pltpu.VMEM),) * 5,
         scratch_shapes=[
-            vmem((share, d), BF16),
+            vmem((2, share, d), BF16),
             vmem((top, tok_rows), jnp.int32),
             vmem((top, tok_rows), F32),
             vmem((total, d), BF16),
@@ -480,8 +534,8 @@
             vmem((n_exp * CHUNK, n_exp * CHUNK), BF16),
             vmem((n_exp * CHUNK, n_exp * CHUNK), BF16),
             vmem((n_exp, CHUNK, LANES), BF16),
+            vmem((n_exp, CHUNK, LANES), BF16),
             vmem((4, n_exp, CHUNK, LANES), BF16),
-            vmem((n_exp * CHUNK, LANES), BF16),
             vmem((LANES, n_exp * CHUNK), BF16),
             vmem((d, total), BF16),
             vmem((d, 4 * 128), BF16),
@@ -503,11 +557,13 @@
             vmem((n_exp, CHUNK, LANES), BF16),
             vmem((n_exp, CHUNK, LANES), BF16),
             vmem((4, share, wide), BF16),
-            vmem((4, rows_z, LANES), BF16),
-            vmem((2, 4, n_dp // 2, rows_z, LANES), BF16),
-            dma((7,)),
-            dma((n_exp,)),
-            dma((n_exp,)),
+            vmem((3, rows_z, LANES), BF16),
+            vmem((rest_rows, 128), BF16),
+            vmem((2, 3, n_dp // 2, rows_z, LANES), BF16),
+            vmem((2, n_dp // 2, rest_rows, 128), BF16),
+            dma((8,)),
+            dma((2, n_exp)),
+            dma((2, n_exp)),
             dma((3, n_exp // 2)),
             dma((3, n_exp // 2)),
             dma((6,)),

time: 93.4 us -> 90.1 us (0.965)
  Pallas kernels: 92.6 us -> 88.9 us
    pallas_call x1, Pallas kernels: 90.4 us -> 86.8 us  [shards(): pl.pallas_call(lambda *refs: kernel((n_dp, n_exp, n_ten, cap, top, d, hid...]
where the time goes in v3:
time: 90.1 us; the launch traced here: 89.6 us
  Pallas kernels  88.9 us (99%)
    pallas_call x1, Pallas kernels, shards(): pl.pallas_call(lambda *refs: kernel((n_dp, n_exp, n_ten, cap, top, d, hid...  86.8 us
    pallas_call x1, Pallas kernels, shards(): pl.pallas_call(finish, out_shape=shapes, in_specs=[pl.BlockSpec(memory_sp...  2.13 us

profile of v3, /device:TPU:1, one launch (start us, length us, event | category | flops | bytes accessed | tf_op | source)
XLA Modules:
  0.0 89.6 jit_solution(16804995464199661877)
XLA Ops:
  0.6 86.8 %expert_backward.1 = (bf16[128,1792]{1,0:T(8,128)(2,1)}, f32[8,128]{1,0:T(8,128)}, f32[320,112]{1,0:T(8,128)}, f32[320,112]{1,0:T(8,128)}, f32[320,112]{1,0:T(8,128)}) custom-call(bf16[128,1792]{1,0:T(8,128)(2,1)} %refs_0_.1, s32[8,128]{1,0:T(8,128)} %bitcast.28, f32[8,128]{1,0:T(8,128)} %bitcast.29, bf16[384,1792]{1,0:T(8,128)(2,1)} %bitcast.24, ...), custom_call_target="tpu_custom_call" | custom-call | tf_op jit(solution)/shard_map/expert_backward/pallas_call | solution.py:518
  87.4 2.1 %write_results.1 = (bf16[128,1792]{1,0:T(8,128)(2,1)}, f32[8,128]{1,0:T(8,128)}, f32[320,112]{1,0:T(8,128)}, f32[320,112]{1,0:T(8,128)}, f32[320,112]{1,0:T(8,128)}) custom-call(bf16[128,1792]{1,0:T(8,128)(2,1)} %get-tuple-element.15.refs_0_, f32[8,128]{1,0:T(8,128)} %get-tuple-element.16.refs_1_, f32[320,112]{1,0:T(8,128)} %get-tuple-element.17.refs_2_, ...), custom_call_target="tpu_custom_call" | custom-call | tf_op jit(solution)/shard_map/write_results/pallas_call | solution.py:591

commit v4 on v3

--- a/solution.py
+++ b/solution.py
@@ -177,6 +177,9 @@
         xcopy(0, i).start()
         xcopy(1, i).start()
 
+    handed = [6, 5, 7, 7]
+    extra = (0, 1, 2)
+
     def hand(i):
         left = i % 2
         m = [members(6), members(5), pl.ds(order[7] * group, 1), pl.ds(order[7] * group + 1, 1)][i]
@@ -186,7 +189,7 @@
         )
 
     def hand_on(i):
-        xcopy(i % 2, [6, 5, 7, 7][i]).wait_recv()
+        xcopy(i % 2, handed[i]).wait_recv()
         hand(i).start()
 
     def forward(first, last):
@@ -239,58 +242,6 @@
     def rows_of(tt):
         return pl.ds(pl.multiple_of(tt * slots, 32), slots)
 
-    def backward(rel, tt):
-        rows = rows_of(tt)
-        opened = dot(unpack[...], recv_buf[rel].reshape(n_exp * CHUNK, LANES))
-
-        def piece(j):
-            return opened[slots * j : slots * (j + 1), :]
-
-        weight = jnp.sum(jnp.where(lane_q, piece(pieces), 0.0), axis=1, keepdims=True)
-        dy = jnp.concatenate([piece(j) for j in range(pieces)], axis=1)
-        at = slice(128 * rel, 128 * (rel + 1))
-        st[:, at] = jnp.concatenate([(weight * dy).astype(BF16), jnp.zeros((blank, d), BF16)], axis=0).T
-        hid_r[at, :] = jnp.concatenate([hid_s[rows, :], jnp.zeros((blank, hid), BF16)], axis=0)
-        back = dot(dy.astype(BF16), wd[...], nt)
-        prob = jnp.sum(hid_s[rows, :].astype(F32) * back, axis=1, keepdims=True)
-        prob_s[rows, :] = jnp.broadcast_to(prob, (slots, 128))
-        hidden_grad = weight * back
-        gate_g[rows, :] = (hidden_grad * slope_up[rows, :]).astype(BF16)
-        up_g[rows, :] = (hidden_grad * silu_s[rows, :]).astype(BF16)
-
-    backward(0, t)
-    hand_on(2)
-    hand_on(3)
-    for i in range(6):
-        xcopy(0, i).wait_recv()
-    backward(1, t_left)
-    for i in (0, 1, 2, 3, 4, 6):
-        xcopy(1, i).wait_recv()
-    backward(2, t_right)
-    for i in range(5):
-        ywait(1, i)
-    for i in range(4):
-        hand(i).wait_recv()
-    backward(3, t_opp)
-    gate_up[...] = jnp.concatenate([gate_g[:, LANES:], up_g[:, LANES:]], axis=1)
-    hid_rest[...] = jnp.concatenate([hid_r[:, LANES:], hid_r[:, LANES:]], axis=1)
-
-    def input_part(tt):
-        rows = rows_of(tt)
-        return dot(gate_g[rows, :], wg[...]) + dot(up_g[rows, :], wu[...])
-
-    def put_part(ref, tt):
-        ref[:, :d] = input_part(tt).astype(BF16)
-        ref[:, d:] = prob_s[rows_of(tt), :].astype(BF16)
-
-    lo, hi = pl.ds(0, half), pl.ds(half, half)
-    first_right = remote(xs_opp.at[lo], xr1.at[0], rsend.at[0], rrecv.at[0], "tensor", t_right)
-    first_left = remote(xs_opp.at[hi], xr1.at[1], rsend.at[1], rrecv.at[1], "tensor", t_left)
-    plain_right = remote(xs_right.at[hi], xr2.at[0, hi], rsend.at[2], rrecv.at[2], "tensor", t_right)
-    plain_left = remote(xs_left.at[lo], xr2.at[1, lo], rsend.at[3], rrecv.at[3], "tensor", t_left)
-    added_right = remote(xs_right.at[lo], xr2.at[0, lo], rsend.at[4], rrecv.at[4], "tensor", t_right)
-    added_left = remote(xs_left.at[hi], xr2.at[1, hi], rsend.at[5], rrecv.at[5], "tensor", t_left)
-
     rows_z = d // n_dp
     hops = n_dp // 2
 
@@ -329,34 +280,113 @@
             parts.append(jnp.concatenate([wide_part[at : at + rows_z, :], folded, pad], axis=0))
         return parts
 
-    def zpiece(s, sub, got):
+    def zpiece(s, sub):
         terms = term(sub, [zrows(0, s), zrows(1, s)])
         for way in range(2):
             total = terms[way]
             slot = zslot(way, sub, s - 1)
-            if got[way]:
-                zcopy(way, sub, s - 1, slot).wait_recv()
-                total = total + slot[...].astype(F32)
-            slot[...] = total.astype(BF16)
+            zcopy(way, sub, s - 1, slot).wait_recv()
+            slot[...] = (total + slot[...].astype(F32)).astype(BF16)
             zcopy(way, sub, s, slot).start()
 
     def zsteps(first, end):
         def step(s, carry):
             for sub in range(4):
-                zpiece(s, sub, (True, True))
+                zpiece(s, sub)
             return carry
 
         lax.fori_loop(first, end, step, 0)
 
-    for sub in (0, 2, 1, 3):
-        zstart(sub)[...] = term(sub, [zrows(0, 0)])[0].astype(BF16)
-        zcopy(sub // 2, sub, 0, zstart(sub)).start()
+    def zfirst_pair(sub):
+        way = sub % 2
+        begin, later = term(sub, [zrows(way, 0), zrows(1 - way, 1)])
+        zstart(sub)[...] = begin.astype(BF16)
+        zcopy(way, sub, 0, zstart(sub)).start()
+        slot = zslot(1 - way, sub, 0)
+        slot[...] = later.astype(BF16)
+        zcopy(1 - way, sub, 1, slot).start()
+
+    def zsecond(sub):
+        way = sub % 2
+        slot = zslot(way, sub, 0)
+        total = term(sub, [zrows(way, 1)])[0]
+        zcopy(way, sub, 0, slot).wait_recv()
+        slot[...] = (total + slot[...].astype(F32)).astype(BF16)
+        zcopy(way, sub, 1, slot).start()
+
+    def opened_block(rel, tt):
+        rows = rows_of(tt)
+        opened = dot(unpack[...], recv_buf[rel].reshape(n_exp * CHUNK, LANES))
+
+        def piece(j):
+            return opened[slots * j : slots * (j + 1), :]
+
+        weight = jnp.sum(jnp.where(lane_q, piece(pieces), 0.0), axis=1, keepdims=True)
+        dy = jnp.concatenate([piece(j) for j in range(pieces)], axis=1)
+        at = slice(128 * rel, 128 * (rel + 1))
+        st[:, at] = jnp.concatenate([(weight * dy).astype(BF16), jnp.zeros((blank, d), BF16)], axis=0).T
+        hid_r[at, :] = jnp.concatenate([hid_s[rows, :], jnp.zeros((blank, hid), BF16)], axis=0)
+
+        def hidden_part():
+            finish_block(rows, dy.astype(BF16), weight)
+
+        return hidden_part
+
+    def finish_block(rows, dy, weight):
+        back = dot(dy, wd[...], nt)
+        prob = jnp.sum(hid_s[rows, :].astype(F32) * back, axis=1, keepdims=True)
+        prob_s[rows, :] = jnp.broadcast_to(prob, (slots, 128))
+        hidden_grad = weight * back
+        gate_g[rows, :] = (hidden_grad * slope_up[rows, :]).astype(BF16)
+        up_g[rows, :] = (hidden_grad * silu_s[rows, :]).astype(BF16)
+
+    def backward(rel, tt):
+        opened_block(rel, tt)()
+
+    backward(0, t)
+    hand_on(2)
+    hand_on(3)
+    for i in range(6):
+        xcopy(0, i).wait_recv()
+    backward(1, t_left)
+    for i in (0, 1, 2, 3, 4, 6):
+        xcopy(1, i).wait_recv()
+    backward(2, t_right)
+    for away in extra:
+        for i in at_distance(away):
+            ywait(1, i)
+    for i in range(4):
+        hand(i).wait_recv()
+    hidden_part = opened_block(3, t_opp)
+    zfirst_pair(2)
+    hidden_part()
+    gate_up[...] = jnp.concatenate([gate_g[:, LANES:], up_g[:, LANES:]], axis=1)
+    hid_rest[...] = jnp.concatenate([hid_r[:, LANES:], hid_r[:, LANES:]], axis=1)
+
+    def input_part(tt):
+        rows = rows_of(tt)
+        return dot(gate_g[rows, :], wg[...]) + dot(up_g[rows, :], wu[...])
+
+    def put_part(ref, tt):
+        ref[:, :d] = input_part(tt).astype(BF16)
+        ref[:, d:] = prob_s[rows_of(tt), :].astype(BF16)
+
+    lo, hi = pl.ds(0, half), pl.ds(half, half)
+    first_right = remote(xs_opp.at[lo], xr1.at[0], rsend.at[0], rrecv.at[0], "tensor", t_right)
+    first_left = remote(xs_opp.at[hi], xr1.at[1], rsend.at[1], rrecv.at[1], "tensor", t_left)
+    plain_right = remote(xs_right.at[hi], xr2.at[0, hi], rsend.at[2], rrecv.at[2], "tensor", t_right)
+    plain_left = remote(xs_left.at[lo], xr2.at[1, lo], rsend.at[3], rrecv.at[3], "tensor", t_left)
+    added_right = remote(xs_right.at[lo], xr2.at[0, lo], rsend.at[4], rrecv.at[4], "tensor", t_right)
+    added_left = remote(xs_left.at[hi], xr2.at[1, hi], rsend.at[5], rrecv.at[5], "tensor", t_left)
+
+    for sub in (1, 0, 3):
+        zfirst_pair(sub)
     put_part(xs_opp, t_opp)
     first_right.start()
     first_left.start()
 
-    for sub in range(4):
-        zpiece(1, sub, (sub < 2, sub >= 2))
+    for sub in (2, 1, 0, 3):
+        zsecond(sub)
     put_part(xs_right, t_right)
     plain_right.start()
     put_part(xs_left, t_left)
@@ -467,7 +497,7 @@
     lax.fori_loop(0, n_exp - 1, sent, 0)
     for away in (0, 4):
         yleft(0, away)
-    for away in range(3):
+    for away in extra:
         yleft(1, away)
     for i in range(groups):
         xcopy(0, i).wait_send()
@@ -480,7 +510,7 @@
         copy.wait_send()
 
     for sub in range(4):
-        zcopy(sub // 2, sub, 0, zstart(sub)).wait_send()
+        zcopy(sub % 2, sub, 0, zstart(sub)).wait_send()
 
     def zsent(s, carry):
         for way in range(2):

time: 90.1 us -> 90.4 us (level)
  no operation moved by 1% of the time
where the time goes in v4:
time: 90.4 us; the launch traced here: 89.7 us
  Pallas kernels  89.1 us (99%)
    pallas_call x1, Pallas kernels, shards(): pl.pallas_call(lambda *refs: kernel((n_dp, n_exp, n_ten, cap, top, d, hid...  86.9 us
    pallas_call x1, Pallas kernels, shards(): pl.pallas_call(finish, out_shape=shapes, in_specs=[pl.BlockSpec(memory_sp...  2.13 us

profile of v4, /device:TPU:1, one launch (start us, length us, event | category | flops | bytes accessed | tf_op | source)
XLA Modules:
  0.0 89.7 jit_solution(8367630547560256362)
XLA Ops:
  0.6 86.9 %expert_backward.1 = (bf16[128,1792]{1,0:T(8,128)(2,1)}, f32[8,128]{1,0:T(8,128)}, f32[320,112]{1,0:T(8,128)}, f32[320,112]{1,0:T(8,128)}, f32[320,112]{1,0:T(8,128)}) custom-call(bf16[128,1792]{1,0:T(8,128)(2,1)} %refs_0_.1, s32[8,128]{1,0:T(8,128)} %bitcast.28, f32[8,128]{1,0:T(8,128)} %bitcast.29, bf16[384,1792]{1,0:T(8,128)(2,1)} %bitcast.24, ...), custom_call_target="tpu_custom_call" | custom-call | tf_op jit(solution)/shard_map/expert_backward/pallas_call | solution.py:548
  87.6 2.1 %write_results.1 = (bf16[128,1792]{1,0:T(8,128)(2,1)}, f32[8,128]{1,0:T(8,128)}, f32[320,112]{1,0:T(8,128)}, f32[320,112]{1,0:T(8,128)}, f32[320,112]{1,0:T(8,128)}) custom-call(bf16[128,1792]{1,0:T(8,128)(2,1)} %get-tuple-element.15.refs_0_, f32[8,128]{1,0:T(8,128)} %get-tuple-element.16.refs_1_, f32[320,112]{1,0:T(8,128)} %get-tuple-element.17.refs_2_, ...), custom_call_target="tpu_custom_call" | custom-call | tf_op jit(solution)/shard_map/write_results/pallas_call | solution.py:621

commit v5 on v4

--- a/solution.py
+++ b/solution.py
@@ -293,6 +293,9 @@
         def step(s, carry):
             for sub in range(4):
                 zpiece(s, sub)
+                if first > 2:
+                    for way in range(2):
+                        zcopy(way, sub, s - 2, zslot(way, sub, s - 2)).wait_send()
             return carry
 
         lax.fori_loop(first, end, step, 0)
@@ -453,6 +456,25 @@
     to_right.start()
     to_left.start()
 
+    def sent(i, carry):
+        wcopy(i).wait_send()
+        return carry
+
+    lax.fori_loop(0, n_exp - 1, sent, 0)
+    for away in (0, 4):
+        yleft(0, away)
+    for away in extra:
+        yleft(1, away)
+    for i in range(groups):
+        xcopy(0, i).wait_send()
+        xcopy(1, i).wait_send()
+    for i in range(4):
+        hand(i).wait_send()
+    for copy in (first_right, first_left, plain_right, plain_left, added_right, added_left):
+        copy.wait_send()
+    for sub in range(4):
+        zcopy(sub % 2, sub, 0, zstart(sub)).wait_send()
+
     def put_tokens(rel, tt):
         rows = pl.ds(pl.multiple_of(tt * share, share), share)
         out_ref[rows, :] = gather[rel, :, :d]
@@ -464,9 +486,9 @@
     on_right.start()
     to_left.wait_recv()
     on_left.start()
-    zsteps(7, hops)
     put_tokens(1, t_left)
     put_tokens(2, t_right)
+    zsteps(7, hops)
     on_right.wait_recv()
     on_left.wait_recv()
     put_tokens(3, t_opp)
@@ -490,27 +512,9 @@
     down_out[LANES:, :] = own[4][:rest]
     prob_out[...] = prob_all[...].T[:top]
 
-    def sent(i, carry):
-        wcopy(i).wait_send()
-        return carry
-
-    lax.fori_loop(0, n_exp - 1, sent, 0)
-    for away in (0, 4):
-        yleft(0, away)
-    for away in extra:
-        yleft(1, away)
-    for i in range(groups):
-        xcopy(0, i).wait_send()
-        xcopy(1, i).wait_send()
-    for i in range(4):
-        hand(i).wait_send()
-    for copy in (first_right, first_left, plain_right, plain_left, added_right, added_left):
-        copy.wait_send()
     for copy in (to_right, to_left, on_right, on_left):
         copy.wait_send()
 
-    for sub in range(4):
-        zcopy(sub % 2, sub, 0, zstart(sub)).wait_send()
 
     def zsent(s, carry):
         for way in range(2):
@@ -518,7 +522,7 @@
                 zcopy(way, sub, s, zslot(way, sub, s)).wait_send()
         return carry
 
-    lax.fori_loop(1, hops, zsent, 0)
+    lax.fori_loop(hops - 2, hops, zsent, 0)
 
 
 def finish(*refs):

time: 90.4 us -> 90.3 us (level)
  no operation moved by 1% of the time
where the time goes in v5:
time: 90.3 us; the launch traced here: 89.3 us
  Pallas kernels  88.7 us (98%)
    pallas_call x1, Pallas kernels, shards(): pl.pallas_call(lambda *refs: kernel((n_dp, n_exp, n_ten, cap, top, d, hid...  86.5 us
    pallas_call x1, Pallas kernels, shards(): pl.pallas_call(finish, out_shape=shapes, in_specs=[pl.BlockSpec(memory_sp...  2.13 us

profile of v5, /device:TPU:1, one launch (start us, length us, event | category | flops | bytes accessed | tf_op | source)
XLA Modules:
  0.0 89.3 jit_solution(15456780781530156795)
XLA Ops:
  0.6 86.5 %expert_backward.1 = (bf16[128,1792]{1,0:T(8,128)(2,1)}, f32[8,128]{1,0:T(8,128)}, f32[320,112]{1,0:T(8,128)}, f32[320,112]{1,0:T(8,128)}, f32[320,112]{1,0:T(8,128)}) custom-call(bf16[128,1792]{1,0:T(8,128)(2,1)} %refs_0_.1, s32[8,128]{1,0:T(8,128)} %bitcast.28, f32[8,128]{1,0:T(8,128)} %bitcast.29, bf16[384,1792]{1,0:T(8,128)(2,1)} %bitcast.24, ...), custom_call_target="tpu_custom_call" | custom-call | tf_op jit(solution)/shard_map/expert_backward/pallas_call | solution.py:552
  87.2 2.1 %write_results.1 = (bf16[128,1792]{1,0:T(8,128)(2,1)}, f32[8,128]{1,0:T(8,128)}, f32[320,112]{1,0:T(8,128)}, f32[320,112]{1,0:T(8,128)}, f32[320,112]{1,0:T(8,128)}) custom-call(bf16[128,1792]{1,0:T(8,128)(2,1)} %get-tuple-element.15.refs_0_, f32[8,128]{1,0:T(8,128)} %get-tuple-element.16.refs_1_, f32[320,112]{1,0:T(8,128)} %get-tuple-element.17.refs_2_, ...), custom_call_target="tpu_custom_call" | custom-call | tf_op jit(solution)/shard_map/write_results/pallas_call | solution.py:625
